TPU v7x, 32 devices: a whole 2x2x4 slice. The times are simulated.
32 devices in a mesh: groups: 2 (over y), gy: 4 (over z), gx: 2 (over x), orb: 2 (over core).
Axes of the slice: x: 2, y: 2, z: 4, core: 2. Of those that a mesh axis runs over, the one named last changes fastest.
Arguments:
- checkpoint: float32 [4, 32, 40, 512], P('groups', 'gy', 'gx', 'orb'), parts along dimension 0, may hold values from -6 to 6
- cotangent: float32 [4, 32, 40, 512], P('groups', 'gy', 'gx', 'orb'), parts along dimension 0, may hold values from -6 to 6
- onsite: float32 [64, 40], P(('groups', 'gy'), 'gx'), parts along dimension 0, may hold values from -1.5 to 1.5
- bond_class: int32 [4, 32, 40], P('groups', 'gy', 'gx'), parts along dimension 0, may hold values from 0 to 15
- bond_table: float32 [16, 4], replicated, may hold values from -3 to 3
- occupied: int32 [1024], P(('groups', 'orb')), parts along dimension 0, may hold values 0 or 1
Outputs:
- adjoint_start: float32 [4, 32, 40, 512], P('groups', 'gy', 'gx', 'orb'), parts along dimension 0
- bond_gradient: float32 [16, 32, 40], P(('groups', 'orb'), 'gy', 'gx'), parts along dimension 0
There are 2 independent parts, one for each index of `groups`. A program takes and returns all parts, laid end to end along the dimension named above; an argument that names none is the same for every part. Nothing has to cross between parts.
All inputs are finite; a program needn't handle non-finite values. No bound on the sum of `occupied` on one device may be relied on, other than what follows from the above.
Results may differ from a plain program's by a relative error of at most 0.00012.
Values sent between devices are 32-bit elements; how exact they have to be, the bound alone decides.
A program may use at most 64 MiB of HBM per device.

v0:
```python
import jax
import jax.numpy as jnp
from jax import lax
from jax.sharding import PartitionSpec as P

time_step = 0.1
half_step = 0.05


def with_halo(x, sides, width):
    for axis, dim in sides:
        count, length = (lax.axis_size(axis), x.shape[dim])
        up = [(i, (i + 1) % count) for i in range(count)]
        down = [(j, i) for i, j in up]
        last = lax.slice_in_dim(x, length - width, length, axis=dim)
        first = lax.slice_in_dim(x, 0, width, axis=dim)
        before = lax.ppermute(last, axis, up)
        after = lax.ppermute(first, axis, down)
        x = jnp.concatenate([before, x, after], axis=dim)
    return x


def passed_along(x, axis, by):
    count = lax.axis_size(axis)
    return lax.ppermute(x, axis, [(i, (i + by) % count) for i in range(count)])


def combine(center, right, left, down, up, mu, bh, bhl, bv, bvu):
    out0 = (
        mu * center[1]
        + bh[0] * right[0]
        + bh[1] * right[1]
        + bv[0] * down[0]
        + bv[1] * down[1]
        - bhl[0] * left[0]
        - bhl[2] * left[1]
        - bvu[0] * up[0]
        - bvu[2] * up[1]
    )
    out1 = (
        -mu * center[0]
        + bh[2] * right[0]
        + bh[3] * right[1]
        + bv[2] * down[0]
        + bv[3] * down[1]
        - bhl[1] * left[0]
        - bhl[3] * left[1]
        - bvu[1] * up[0]
        - bvu[3] * up[1]
    )
    return jnp.stack([out0, out1])


def generator(padded, coef):
    center = padded[:, 1:-1, 1:-1]
    right = padded[:, 1:-1, 2:]
    left = padded[:, 1:-1, :-2]
    down = padded[:, 2:, 1:-1]
    upper = padded[:, :-2, 1:-1]
    mu = coef[0, 1:-1, 1:-1][:, :, None]
    bh = coef[1:5, 1:-1, 1:-1][:, :, :, None]
    bhl = coef[1:5, 1:-1, :-2][:, :, :, None]
    bv = coef[5:9, 1:-1, 1:-1][:, :, :, None]
    bvu = coef[5:9, :-2, 1:-1][:, :, :, None]
    return combine(center, right, left, down, upper, mu, bh, bhl, bv, bvu)


def pair_grad(lam_pad, val_pad):
    hp = lax.Precision.HIGHEST
    lam = lam_pad[:, 1:-1, 1:-1]
    val = val_pad[:, 1:-1, 1:-1]
    lam_r = lam_pad[:, 1:-1, 2:]
    val_r = val_pad[:, 1:-1, 2:]
    lam_d = lam_pad[:, 2:, 1:-1]
    val_d = val_pad[:, 2:, 1:-1]
    horiz = jnp.einsum("aijk,bijk->abij", lam, val_r, precision=hp) - jnp.einsum(
        "aijk,bijk->abij", val, lam_r, precision=hp
    )
    vert = jnp.einsum("aijk,bijk->abij", lam, val_d, precision=hp) - jnp.einsum(
        "aijk,bijk->abij", val, lam_d, precision=hp
    )
    rows, cols = (lam.shape[1], lam.shape[2])
    return jnp.concatenate([horiz.reshape(4, rows, cols), vert.reshape(4, rows, cols)], axis=0)


def padded_once(field):
    return with_halo(field, (("gy", 1), ("gx", 2)), 1)


def two_sections(field, coef_near, first, keep):
    near = padded_once(field)
    moved = generator(near, coef_near)
    if keep:
        middle = field + first * moved
    else:
        middle = first * moved
    mid_near = padded_once(middle)
    return (near, mid_near)


def on_device(checkpoint, cotangent, onsite, bond_class, bond_table, occupied):
    classes = bond_table.shape[0]
    rows, cols = onsite.shape
    onehot = (bond_class[:, :, :, None] == jnp.arange(classes, dtype=jnp.int32)).astype(jnp.float32)
    looked = jnp.einsum("dijn,ne->deij", onehot, bond_table, precision=lax.Precision.HIGHEST)
    coef = jnp.concatenate([onsite[None], looked.reshape(8, rows, cols)], axis=0)
    left_col = passed_along(coef[:, :, -1:], "gx", 1)
    up_row = passed_along(coef[:, -1:, :], "gy", 1)
    spare_col = jnp.zeros((coef.shape[0], rows, 1), jnp.float32)
    spare_dot = jnp.zeros((coef.shape[0], 1, 1), jnp.float32)
    middle_band = jnp.concatenate([left_col, coef, spare_col], axis=2)
    top_band = jnp.concatenate([spare_dot, up_row, spare_dot], axis=2)
    bottom_band = jnp.zeros((coef.shape[0], 1, cols + 2), jnp.float32)
    coef_near = jnp.concatenate([top_band, middle_band, bottom_band], axis=1)
    x0p, y0p = two_sections(checkpoint, coef_near, half_step, True)
    x1 = checkpoint + time_step * generator(y0p, coef_near)
    x1p, y1p = two_sections(x1, coef_near, half_step, True)
    signs = (2 * occupied - 1).astype(jnp.float32)
    l2 = cotangent * signs[None, None, None, :]
    l2p, ly1p = two_sections(l2, coef_near, -time_step, False)
    ly1 = ly1p[:, 1:-1, 1:-1]
    l1 = l2 + ly1 - half_step * generator(ly1p, coef_near)
    late = time_step * pair_grad(l2p, y1p) + half_step * pair_grad(ly1p, x1p)
    l1p, ly0p = two_sections(l1, coef_near, -time_step, False)
    ly0 = ly0p[:, 1:-1, 1:-1]
    adjoint_start = l1 + ly0 - half_step * generator(ly0p, coef_near)
    early = time_step * pair_grad(l1p, y0p) + half_step * pair_grad(ly0p, x0p)
    bond_gradient = lax.psum_scatter(
        late, "orb", scatter_dimension=0, tiled=True
    ) + lax.psum_scatter(early, "orb", scatter_dimension=0, tiled=True)
    return (adjoint_start, bond_gradient)


def solution(mesh):
    in_specs = (
        P("groups", "gy", "gx", "orb"),
        P("groups", "gy", "gx", "orb"),
        P(("groups", "gy"), "gx"),
        P("groups", "gy", "gx"),
        P(),
        P(("groups", "orb")),
    )
    out_specs = (P("groups", "gy", "gx", "orb"), P(("groups", "orb"), "gy", "gx"))
    return jax.shard_map(
        on_device, mesh=mesh, in_specs=in_specs, out_specs=out_specs, check_vma=False
    )
```

profile of v0, /device:TPU:0, one launch (start us, length us, event | category | flops | bytes accessed | tf_op | source)
XLA Modules:
  0.0 155.5 jit_solution(14003471071650936918)
XLA Ops:
  9.2 5.1 %collective-permute-start.1 = (f32[2,1,20,256]{3,0,2,1:T(2,128)S(1)}, f32[2,1,20,256]{3,0,2,1:T(2,128)S(1)}, u32[]{:S(2)}, u32[]{:S(2)}) collective-permute-start(f32[2,1,20,256]{3,0,2,1:T(2,128)S(1)} %get-tuple-element.41), channel_id=1, source_target_pairs={{4,0},{8,4},{12,8},{0,12},{5,1},{9,5},{13,9},{1,13},{6,2},{10,6},{... | collective-permute-start | bytes 122888 | tf_op jit(solution)/shard_map/ppermute | solution.py:18
  18.6 3.8 %collective-permute-start.19 = (f32[2,1,20,256]{3,0,2,1:T(2,128)S(1)}, f32[2,1,20,256]{3,0,2,1:T(2,128)S(1)}, u32[]{:S(2)}, u32[]{:S(2)}) collective-permute-start(f32[2,1,20,256]{3,0,2,1:T(2,128)S(1)} %get-tuple-element.32), channel_id=1, source_target_pairs={{4,0},{8,4},{12,8},{0,12},{5,1},{9,5},{13,9},{1,13},{6,2},{10,6},{... | collective-permute-start | bytes 122888 | tf_op jit(solution)/shard_map/ppermute | solution.py:18
  28.0 2.2 %multiply_subtract_fusion.13 = f32[1,8,20,256]{3,0,2,1:T(1,128)S(1)} fusion(f32[2,8,20,256]{3,0,2,1:T(2,128)S(1)} %copy_multiply_fusion, f32[8,20]{1,0:T(8,128)S(1)} %get-tuple-element.49, f32[8,20]{1,0:T(8,128)S(1)} %get-tuple-element.46, f32[8,20]{1,0:T(8,128)S(1)} %get-tuple-element.44, f32[8,20]{1,0:T(8,128)S(1)} %get-tuple-element.42, ...), kind=kLoop, calls=%fused_computation.193 | loop fusion | flops 1351680 | bytes 815104 | tf_op jit(solution)/shard_map/sub | solution.py:30
  30.2 2.2 %multiply_subtract_fusion.12 = f32[1,8,20,256]{3,0,2,1:T(1,128)S(1)} fusion(f32[2,8,20,256]{3,0,2,1:T(2,128)S(1)} %copy_multiply_fusion, f32[8,20]{1,0:T(8,128)S(1)} %get-tuple-element.47, f32[8,20]{1,0:T(8,128)S(1)} %get-tuple-element.48, f32[8,20]{1,0:T(8,128)S(1)} %get-tuple-element.45, f32[8,20]{1,0:T(8,128)S(1)} %get-tuple-element.43, ...), kind=kLoop, calls=%fused_computation.192 | loop fusion | flops 1351680 | bytes 815104 | tf_op jit(solution)/shard_map/sub | solution.py:41
  34.0 3.8 %collective-permute-start.7 = (f32[2,1,20,256]{3,0,2,1:T(2,128)S(1)}, f32[2,1,20,256]{3,0,2,1:T(2,128)S(1)}, u32[]{:S(2)}, u32[]{:S(2)}) collective-permute-start(f32[2,1,20,256]{3,0,2,1:T(2,128)S(1)} %get-tuple-element.39), channel_id=1, source_target_pairs={{4,0},{8,4},{12,8},{0,12},{5,1},{9,5},{13,9},{1,13},{6,2},{10,6},{... | collective-permute-start | bytes 122888 | tf_op jit(solution)/shard_map/ppermute | solution.py:18
  37.7 2.1 %multiply_subtract_fusion.5 = f32[1,8,20,256]{3,0,2,1:T(1,128)S(1)} fusion(f32[1,8,20,256]{3,1,2,0:T(8,128)S(1)} %get-tuple-element.28, f32[2,9,20,256]{3,0,2,1:T(2,128)S(1)} %get-tuple-element.31, f32[2,9,20,256]{3,0,2,1:T(2,128)S(1)} %get-tuple-element.51, f32[8,20]{1,0:T(8,128)S(1)} %get-tuple-element.49, f32[8,20]{1,0:T(8,128)S(1)} %get-tuple-element.46, ...), kind=kLoop, calls=%fused_computation.184 | loop fusion | flops 819200 | bytes 1438720 | tf_op jit(solution)/shard_map/sub | solution.py:30
  39.9 2.1 %multiply_subtract_fusion.4 = f32[1,8,20,256]{3,0,2,1:T(1,128)S(1)} fusion(f32[1,8,20,256]{3,1,2,0:T(8,128)S(1)} %get-tuple-element.29, f32[2,9,20,256]{3,0,2,1:T(2,128)S(1)} %get-tuple-element.31, f32[2,9,20,256]{3,0,2,1:T(2,128)S(1)} %get-tuple-element.51, f32[8,20]{1,0:T(8,128)S(1)} %get-tuple-element.47, f32[8,20]{1,0:T(8,128)S(1)} %get-tuple-element.48, ...), kind=kLoop, calls=%fused_computation.182 | loop fusion | flops 819200 | bytes 1438720 | tf_op jit(solution)/shard_map/sub | solution.py:41
  42.5 3.8 %collective-permute-start.23 = (f32[2,1,20,256]{3,0,2,1:T(2,128)S(1)}, f32[2,1,20,256]{3,0,2,1:T(2,128)S(1)}, u32[]{:S(2)}, u32[]{:S(2)}) collective-permute-start(f32[2,1,20,256]{3,0,2,1:T(2,128)S(1)} %get-tuple-element.27), channel_id=1, source_target_pairs={{4,0},{8,4},{12,8},{0,12},{5,1},{9,5},{13,9},{1,13},{6,2},{10,6},{... | collective-permute-start | bytes 122888 | tf_op jit(solution)/shard_map/ppermute | solution.py:18
  51.1 2.2 %multiply_subtract_fusion.11 = f32[1,8,20,256]{3,0,2,1:T(1,128)S(1)} fusion(f32[2,8,20,256]{3,0,2,1:T(2,128)S(1)} %maximum_multiply_fusion, f32[8,20]{1,0:T(8,128)S(1)} %get-tuple-element.49, f32[8,20]{1,0:T(8,128)S(1)} %get-tuple-element.46, f32[8,20]{1,0:T(8,128)S(1)} %get-tuple-element.44, f32[8,20]{1,0:T(8,128)S(1)} %get-tuple-element.42, ...), kind=kLoop, calls=%fused_computation.191 | loop fusion | flops 1351680 | bytes 815104 | tf_op jit(solution)/shard_map/sub | solution.py:30
  53.3 2.2 %multiply_subtract_fusion.10 = f32[1,8,20,256]{3,0,2,1:T(1,128)S(1)} fusion(f32[2,8,20,256]{3,0,2,1:T(2,128)S(1)} %maximum_multiply_fusion, f32[8,20]{1,0:T(8,128)S(1)} %get-tuple-element.47, f32[8,20]{1,0:T(8,128)S(1)} %get-tuple-element.48, f32[8,20]{1,0:T(8,128)S(1)} %get-tuple-element.45, f32[8,20]{1,0:T(8,128)S(1)} %get-tuple-element.43, ...), kind=kLoop, calls=%fused_computation.190 | loop fusion | flops 1351680 | bytes 815104 | tf_op jit(solution)/shard_map/sub | solution.py:41
  56.5 4.0 %collective-permute-start.11 = (f32[2,1,20,256]{3,0,2,1:T(2,128)S(1)}, f32[2,1,20,256]{3,0,2,1:T(2,128)S(1)}, u32[]{:S(2)}, u32[]{:S(2)}) collective-permute-start(f32[2,1,20,256]{3,0,2,1:T(2,128)S(1)} %get-tuple-element.37), channel_id=1, source_target_pairs={{4,0},{8,4},{12,8},{0,12},{5,1},{9,5},{13,9},{1,13},{6,2},{10,6},{... | collective-permute-start | bytes 122888 | tf_op jit(solution)/shard_map/ppermute | solution.py:18
  60.5 2.2 %multiply_subtract_fusion.3 = f32[1,8,20,256]{3,0,2,1:T(1,128)S(1)} fusion(f32[2,8,20,256]{3,0,2,1:T(2,128)S(1)} %fusion.37, f32[8,20]{1,0:T(8,128)S(1)} %get-tuple-element.49, f32[8,20]{1,0:T(8,128)S(1)} %get-tuple-element.46, f32[8,20]{1,0:T(8,128)S(1)} %get-tuple-element.44, f32[8,20]{1,0:T(8,128)S(1)} %get-tuple-element.42, f32[8,20]{1,0:T(8,128)S(1)} %bitcast.131, ...), kind=kLoop, calls=%fused_computation.181 | loop fusion | flops 1351680 | bytes 815104 | tf_op jit(solution)/shard_map/sub | solution.py:30
  62.8 2.2 %multiply_subtract_fusion.2 = f32[1,8,20,256]{3,0,2,1:T(1,128)S(1)} fusion(f32[2,8,20,256]{3,0,2,1:T(2,128)S(1)} %fusion.37, f32[8,20]{1,0:T(8,128)S(1)} %get-tuple-element.47, f32[8,20]{1,0:T(8,128)S(1)} %get-tuple-element.48, f32[8,20]{1,0:T(8,128)S(1)} %get-tuple-element.45, f32[8,20]{1,0:T(8,128)S(1)} %get-tuple-element.43, f32[8,20]{1,0:T(8,128)S(1)} %bitcast.96, ...), kind=kLoop, calls=%fused_computation.180 | loop fusion | flops 1351680 | bytes 815104 | tf_op jit(solution)/shard_map/sub | solution.py:41
  67.6 3.8 %collective-permute-start.27 = (f32[2,1,20,256]{3,0,2,1:T(2,128)S(1)}, f32[2,1,20,256]{3,0,2,1:T(2,128)S(1)}, u32[]{:S(2)}, u32[]{:S(2)}) collective-permute-start(f32[2,1,20,256]{3,0,2,1:T(2,128)S(1)} %get-tuple-element.25), channel_id=1, source_target_pairs={{4,0},{8,4},{12,8},{0,12},{5,1},{9,5},{13,9},{1,13},{6,2},{10,6},{... | collective-permute-start | bytes 122888 | tf_op jit(solution)/shard_map/ppermute | solution.py:18
  71.5 2.1 %fusion.33 = f32[8,20,2,2]{3,2,1,0:T(2,128)} fusion(f32[2,8,20,256]{3,0,2,1:T(2,128)S(1)} %fusion.38, f32[2,1,20,256]{3,0,2,1:T(2,128)S(1)} %collective-permute-done.7, f32[2,8,20,256]{3,0,2,1:T(2,128)S(1)} %maximum_multiply_fusion), kind=kOutput, calls=%fused_computation.57 | convolution fusion | flops 2058240 | bytes 698880 | tf_op jit(solution)/shard_map/aijk,bijk->abij/dot_general | solution.py:79
  85.4 2.2 %multiply_subtract_fusion.9 = f32[1,8,20,256]{3,0,2,1:T(1,128)S(1)} fusion(f32[2,8,20,256]{3,0,2,1:T(2,128)S(1)} %fusion.35, f32[8,20]{1,0:T(8,128)S(1)} %get-tuple-element.49, f32[8,20]{1,0:T(8,128)S(1)} %get-tuple-element.46, f32[8,20]{1,0:T(8,128)S(1)} %get-tuple-element.44, f32[8,20]{1,0:T(8,128)S(1)} %get-tuple-element.42, f32[8,20]{1,0:T(8,128)S(1)} %bitcast.132, ...), kind=kLoop, calls=%fused_computation.189 | loop fusion | flops 1351680 | bytes 815104 | tf_op jit(solution)/shard_map/sub | solution.py:30
  87.6 2.2 %multiply_subtract_fusion.8 = f32[1,8,20,256]{3,0,2,1:T(1,128)S(1)} fusion(f32[2,8,20,256]{3,0,2,1:T(2,128)S(1)} %fusion.35, f32[8,20]{1,0:T(8,128)S(1)} %get-tuple-element.47, f32[8,20]{1,0:T(8,128)S(1)} %get-tuple-element.48, f32[8,20]{1,0:T(8,128)S(1)} %get-tuple-element.45, f32[8,20]{1,0:T(8,128)S(1)} %get-tuple-element.43, f32[8,20]{1,0:T(8,128)S(1)} %bitcast.97, ...), kind=kLoop, calls=%fused_computation.188 | loop fusion | flops 1351680 | bytes 815104 | tf_op jit(solution)/shard_map/sub | solution.py:41
  91.9 12.8 %collective-permute-start.14 = (f32[2,1,20,256]{3,0,2,1:T(2,128)}, f32[2,1,20,256]{3,0,2,1:T(2,128)S(1)}, u32[]{:S(2)}, u32[]{:S(2)}) collective-permute-start(f32[2,1,20,256]{3,0,2,1:T(2,128)} %get-tuple-element.34), channel_id=1, source_target_pairs={{0,4},{4,8},{8,12},{12,0},{1,5},{5,9},{9,13},{13,1},{2,6},{6,10},{... | collective-permute-start | bytes 122888 | tf_op jit(solution)/shard_map/ppermute | solution.py:17
  104.8 3.8 %collective-permute-start.15 = (f32[2,1,20,256]{3,0,2,1:T(2,128)S(1)}, f32[2,1,20,256]{3,0,2,1:T(2,128)S(1)}, u32[]{:S(2)}, u32[]{:S(2)}) collective-permute-start(f32[2,1,20,256]{3,0,2,1:T(2,128)S(1)} %get-tuple-element.35), channel_id=1, source_target_pairs={{4,0},{8,4},{12,8},{0,12},{5,1},{9,5},{13,9},{1,13},{6,2},{10,6},{... | collective-permute-start | bytes 122888 | tf_op jit(solution)/shard_map/ppermute | solution.py:18
  113.4 2.2 %multiply_subtract_fusion.1 = f32[1,8,20,256]{3,0,2,1:T(1,128)S(1)} fusion(f32[2,8,20,256]{3,0,2,1:T(2,128)S(1)} %fusion.38, f32[8,20]{1,0:T(8,128)S(1)} %get-tuple-element.49, f32[8,20]{1,0:T(8,128)S(1)} %get-tuple-element.46, f32[8,20]{1,0:T(8,128)S(1)} %get-tuple-element.44, f32[8,20]{1,0:T(8,128)S(1)} %get-tuple-element.42, f32[8,20]{1,0:T(8,128)S(1)} %bitcast.133, ...), kind=kLoop, calls=%fused_computation.179 | loop fusion | flops 1351680 | bytes 815104 | tf_op jit(solution)/shard_map/sub | solution.py:30
  115.6 2.2 %multiply_subtract_fusion = f32[1,8,20,256]{3,0,2,1:T(1,128)S(1)} fusion(f32[2,8,20,256]{3,0,2,1:T(2,128)S(1)} %fusion.38, f32[8,20]{1,0:T(8,128)S(1)} %get-tuple-element.47, f32[8,20]{1,0:T(8,128)S(1)} %get-tuple-element.48, f32[8,20]{1,0:T(8,128)S(1)} %get-tuple-element.45, f32[8,20]{1,0:T(8,128)S(1)} %get-tuple-element.43, f32[8,20]{1,0:T(8,128)S(1)} %bitcast.98, ...), kind=kLoop, calls=%fused_computation.178 | loop fusion | flops 1351680 | bytes 815104 | tf_op jit(solution)/shard_map/sub | solution.py:41
  118.6 3.8 %collective-permute-start.31 = (f32[2,1,20,256]{3,0,2,1:T(2,128)S(1)}, f32[2,1,20,256]{3,0,2,1:T(2,128)S(1)}, u32[]{:S(2)}, u32[]{:S(2)}) collective-permute-start(f32[2,1,20,256]{3,0,2,1:T(2,128)S(1)} %get-tuple-element.23), channel_id=1, source_target_pairs={{4,0},{8,4},{12,8},{0,12},{5,1},{9,5},{13,9},{1,13},{6,2},{10,6},{... | collective-permute-start | bytes 122888 | tf_op jit(solution)/shard_map/ppermute | solution.py:18
  141.6 2.2 %multiply_subtract_fusion.7 = f32[1,8,20,256]{3,0,2,1:T(1,128)S(1)} fusion(f32[2,8,20,256]{3,0,2,1:T(2,128)S(1)} %maximum_multiply_fusion.2, f32[8,20]{1,0:T(8,128)S(1)} %get-tuple-element.49, f32[8,20]{1,0:T(8,128)S(1)} %get-tuple-element.46, f32[8,20]{1,0:T(8,128)S(1)} %get-tuple-element.44, f32[8,20]{1,0:T(8,128)S(1)} %get-tuple-element.42, ...), kind=kLoop, calls=%fused_computation.187 | loop fusion | flops 1351680 | bytes 815104 | tf_op jit(solution)/shard_map/sub | solution.py:30
  143.9 2.2 %multiply_subtract_fusion.6 = f32[1,8,20,256]{3,0,2,1:T(1,128)S(1)} fusion(f32[2,8,20,256]{3,0,2,1:T(2,128)S(1)} %maximum_multiply_fusion.2, f32[8,20]{1,0:T(8,128)S(1)} %get-tuple-element.47, f32[8,20]{1,0:T(8,128)S(1)} %get-tuple-element.48, f32[8,20]{1,0:T(8,128)S(1)} %get-tuple-element.45, f32[8,20]{1,0:T(8,128)S(1)} %get-tuple-element.43, ...), kind=kLoop, calls=%fused_computation.186 | loop fusion | flops 1351680 | bytes 815104 | tf_op jit(solution)/shard_map/sub | solution.py:41
  (197 shorter events, 62.8 us)
Async XLA Ops:
  7.2 141.3 %reduce-scatter.2.cloned.1.call-start = ((), (), s32[]{:S(2)}) async-start(), calls=%async_computation.1 | async-start | bytes 49152 | tf_op jit(solution)/shard_map/reduce_scatter | solution.py:128
  9.2 13.4 %collective-permute-start.1 = (f32[2,1,20,256]{3,0,2,1:T(2,128)S(1)}, f32[2,1,20,256]{3,0,2,1:T(2,128)S(1)}, u32[]{:S(2)}, u32[]{:S(2)}) collective-permute-start(f32[2,1,20,256]{3,0,2,1:T(2,128)S(1)} %get-tuple-element.41), channel_id=1, source_target_pairs={{4,0},{8,4},{12,8},{0,12},{5,1},{9,5},{13,9},{1,13},{6,2},{10,6},{... | collective-permute-start | bytes 122888 | tf_op jit(solution)/shard_map/ppermute | solution.py:18
  14.3 8.3 %collective-permute-start = (f32[2,1,20,256]{3,0,2,1:T(2,128)S(1)}, f32[2,1,20,256]{3,0,2,1:T(2,128)S(1)}, u32[]{:S(2)}, u32[]{:S(2)}) collective-permute-start(f32[2,1,20,256]{3,0,2,1:T(2,128)S(1)} %get-tuple-element.40), channel_id=1, source_target_pairs={{0,4},{4,8},{8,12},{12,0},{1,5},{5,9},{9,13},{13,1},{2,6},{6,10},{... | collective-permute-start | bytes 122888 | tf_op jit(solution)/shard_map/ppermute | solution.py:17
  16.5 8.2 %collective-permute-start.18 = (f32[2,1,20,256]{3,0,2,1:T(2,128)S(1)}, f32[2,1,20,256]{3,0,2,1:T(2,128)S(1)}, u32[]{:S(2)}, u32[]{:S(2)}) collective-permute-start(f32[2,1,20,256]{3,0,2,1:T(2,128)S(1)} %get-tuple-element.33), channel_id=1, source_target_pairs={{0,4},{4,8},{8,12},{12,0},{1,5},{5,9},{9,13},{13,1},{2,6},{6,10},{... | collective-permute-start | bytes 122888 | tf_op jit(solution)/shard_map/ppermute | solution.py:17
  25.1 12.6 %collective-permute-start.20 = (f32[2,10,1,256]{3,0,2,1:T(2,128)S(1)}, f32[2,10,1,256]{3,0,2,1:T(2,128)S(1)}, u32[]{:S(2)}, u32[]{:S(2)}) collective-permute-start(f32[2,10,1,256]{3,0,2,1:T(2,128)S(1)} %get-tuple-element.13), channel_id=1, source_target_pairs={{2,0},{0,2},{3,1},{1,3},{6,4},{4,6},{7,5},{5,7},{10,8},{8,10},{11,... | collective-permute-start | bytes 61448 | tf_op jit(solution)/shard_map/ppermute | solution.py:18
  26.7 11.1 %collective-permute-start.21 = (f32[2,10,1,256]{3,0,2,1:T(2,128)S(1)}, f32[2,10,1,256]{3,0,2,1:T(2,128)S(1)}, u32[]{:S(2)}, u32[]{:S(2)}) collective-permute-start(f32[2,10,1,256]{3,0,2,1:T(2,128)S(1)} %get-tuple-element.12), channel_id=1, source_target_pairs={{0,2},{2,0},{1,3},{3,1},{4,6},{6,4},{5,7},{7,5},{8,10},{10,8},{9,1... | collective-permute-start | bytes 61448 | tf_op jit(solution)/shard_map/ppermute | solution.py:17
  33.9 12.6 %collective-permute-start.6 = (f32[2,1,20,256]{3,0,2,1:T(2,128)S(1)}, f32[2,1,20,256]{3,0,2,1:T(2,128)S(1)}, u32[]{:S(2)}, u32[]{:S(2)}) collective-permute-start(f32[2,1,20,256]{3,0,2,1:T(2,128)S(1)} %get-tuple-element.38), channel_id=1, source_target_pairs={{0,4},{4,8},{8,12},{12,0},{1,5},{5,9},{9,13},{13,1},{2,6},{6,10},{... | collective-permute-start | bytes 122888 | tf_op jit(solution)/shard_map/ppermute | solution.py:17
  34.0 12.5 %collective-permute-start.7 = (f32[2,1,20,256]{3,0,2,1:T(2,128)S(1)}, f32[2,1,20,256]{3,0,2,1:T(2,128)S(1)}, u32[]{:S(2)}, u32[]{:S(2)}) collective-permute-start(f32[2,1,20,256]{3,0,2,1:T(2,128)S(1)} %get-tuple-element.39), channel_id=1, source_target_pairs={{4,0},{8,4},{12,8},{0,12},{5,1},{9,5},{13,9},{1,13},{6,2},{10,6},{... | collective-permute-start | bytes 122888 | tf_op jit(solution)/shard_map/ppermute | solution.py:18
  48.7 11.9 %collective-permute-start.24 = (f32[2,10,1,256]{3,0,2,1:T(2,128)S(1)}, f32[2,10,1,256]{3,0,2,1:T(2,128)S(1)}, u32[]{:S(2)}, u32[]{:S(2)}) collective-permute-start(f32[2,10,1,256]{3,0,2,1:T(2,128)S(1)} %get-tuple-element.11), channel_id=1, source_target_pairs={{2,0},{0,2},{3,1},{1,3},{6,4},{4,6},{7,5},{5,7},{10,8},{8,10},{11,... | collective-permute-start | bytes 61448 | tf_op jit(solution)/shard_map/ppermute | solution.py:18
  49.4 11.1 %collective-permute-start.25 = (f32[2,10,1,256]{3,0,2,1:T(2,128)S(1)}, f32[2,10,1,256]{3,0,2,1:T(2,128)S(1)}, u32[]{:S(2)}, u32[]{:S(2)}) collective-permute-start(f32[2,10,1,256]{3,0,2,1:T(2,128)S(1)} %get-tuple-element.10), channel_id=1, source_target_pairs={{0,2},{2,0},{1,3},{3,1},{4,6},{6,4},{5,7},{7,5},{8,10},{10,8},{9,1... | collective-permute-start | bytes 61448 | tf_op jit(solution)/shard_map/ppermute | solution.py:17
  56.4 18.1 %collective-permute-start.10 = (f32[2,1,20,256]{3,0,2,1:T(2,128)S(1)}, f32[2,1,20,256]{3,0,2,1:T(2,128)S(1)}, u32[]{:S(2)}, u32[]{:S(2)}) collective-permute-start(f32[2,1,20,256]{3,0,2,1:T(2,128)S(1)} %get-tuple-element.36), channel_id=1, source_target_pairs={{0,4},{4,8},{8,12},{12,0},{1,5},{5,9},{9,13},{13,1},{2,6},{6,10},{... | collective-permute-start | bytes 122888 | tf_op jit(solution)/shard_map/ppermute | solution.py:17
  56.5 18.0 %collective-permute-start.11 = (f32[2,1,20,256]{3,0,2,1:T(2,128)S(1)}, f32[2,1,20,256]{3,0,2,1:T(2,128)S(1)}, u32[]{:S(2)}, u32[]{:S(2)}) collective-permute-start(f32[2,1,20,256]{3,0,2,1:T(2,128)S(1)} %get-tuple-element.37), channel_id=1, source_target_pairs={{4,0},{8,4},{12,8},{0,12},{5,1},{9,5},{13,9},{1,13},{6,2},{10,6},{... | collective-permute-start | bytes 122888 | tf_op jit(solution)/shard_map/ppermute | solution.py:18
  67.6 12.6 %collective-permute-start.26 = (f32[2,1,20,256]{3,0,2,1:T(2,128)S(1)}, f32[2,1,20,256]{3,0,2,1:T(2,128)S(1)}, u32[]{:S(2)}, u32[]{:S(2)}) collective-permute-start(f32[2,1,20,256]{3,0,2,1:T(2,128)S(1)} %get-tuple-element.24), channel_id=1, source_target_pairs={{0,4},{4,8},{8,12},{12,0},{1,5},{5,9},{9,13},{13,1},{2,6},{6,10},{... | collective-permute-start | bytes 122888 | tf_op jit(solution)/shard_map/ppermute | solution.py:17
  67.6 12.6 %collective-permute-start.27 = (f32[2,1,20,256]{3,0,2,1:T(2,128)S(1)}, f32[2,1,20,256]{3,0,2,1:T(2,128)S(1)}, u32[]{:S(2)}, u32[]{:S(2)}) collective-permute-start(f32[2,1,20,256]{3,0,2,1:T(2,128)S(1)} %get-tuple-element.25), channel_id=1, source_target_pairs={{4,0},{8,4},{12,8},{0,12},{5,1},{9,5},{13,9},{1,13},{6,2},{10,6},{... | collective-permute-start | bytes 122888 | tf_op jit(solution)/shard_map/ppermute | solution.py:18
  74.5 10.9 %collective-permute-start.12 = (f32[2,10,1,256]{3,0,2,1:T(2,128)S(1)}, f32[2,10,1,256]{3,0,2,1:T(2,128)S(1)}, u32[]{:S(2)}, u32[]{:S(2)}) collective-permute-start(f32[2,10,1,256]{3,0,2,1:T(2,128)S(1)} %get-tuple-element.17), channel_id=1, source_target_pairs={{2,0},{0,2},{3,1},{1,3},{6,4},{4,6},{7,5},{5,7},{10,8},{8,10},{11,... | collective-permute-start | bytes 61448 | tf_op jit(solution)/shard_map/ppermute | solution.py:18
  75.9 9.5 %collective-permute-start.13 = (f32[2,10,1,256]{3,0,2,1:T(2,128)S(1)}, f32[2,10,1,256]{3,0,2,1:T(2,128)S(1)}, u32[]{:S(2)}, u32[]{:S(2)}) collective-permute-start(f32[2,10,1,256]{3,0,2,1:T(2,128)S(1)} %get-tuple-element.16), channel_id=1, source_target_pairs={{0,2},{2,0},{1,3},{3,1},{4,6},{6,4},{5,7},{7,5},{8,10},{10,8},{9,1... | collective-permute-start | bytes 61448 | tf_op jit(solution)/shard_map/ppermute | solution.py:17
  80.9 29.3 %collective-permute-start.28 = (f32[2,10,1,256]{3,0,2,1:T(2,128)}, f32[2,10,1,256]{3,0,2,1:T(2,128)S(1)}, u32[]{:S(2)}, u32[]{:S(2)}) collective-permute-start(f32[2,10,1,256]{3,0,2,1:T(2,128)} %get-tuple-element.9), channel_id=1, source_target_pairs={{2,0},{0,2},{3,1},{1,3},{6,4},{4,6},{7,5},{5,7},{10,8},{8,10},{11,... | collective-permute-start | bytes 61448 | tf_op jit(solution)/shard_map/ppermute | solution.py:18
  84.8 28.7 %collective-permute-start.29 = (f32[2,10,1,256]{3,0,2,1:T(2,128)S(1)}, f32[2,10,1,256]{3,0,2,1:T(2,128)S(1)}, u32[]{:S(2)}, u32[]{:S(2)}) collective-permute-start(f32[2,10,1,256]{3,0,2,1:T(2,128)S(1)} %get-tuple-element.8), channel_id=1, source_target_pairs={{0,2},{2,0},{1,3},{3,1},{4,6},{6,4},{5,7},{7,5},{8,10},{10,8},{9,1... | collective-permute-start | bytes 61448 | tf_op jit(solution)/shard_map/ppermute | solution.py:17
  91.9 34.0 %collective-permute-start.14 = (f32[2,1,20,256]{3,0,2,1:T(2,128)}, f32[2,1,20,256]{3,0,2,1:T(2,128)S(1)}, u32[]{:S(2)}, u32[]{:S(2)}) collective-permute-start(f32[2,1,20,256]{3,0,2,1:T(2,128)} %get-tuple-element.34), channel_id=1, source_target_pairs={{0,4},{4,8},{8,12},{12,0},{1,5},{5,9},{9,13},{13,1},{2,6},{6,10},{... | collective-permute-start | bytes 122888 | tf_op jit(solution)/shard_map/ppermute | solution.py:17
  104.8 21.2 %collective-permute-start.15 = (f32[2,1,20,256]{3,0,2,1:T(2,128)S(1)}, f32[2,1,20,256]{3,0,2,1:T(2,128)S(1)}, u32[]{:S(2)}, u32[]{:S(2)}) collective-permute-start(f32[2,1,20,256]{3,0,2,1:T(2,128)S(1)} %get-tuple-element.35), channel_id=1, source_target_pairs={{4,0},{8,4},{12,8},{0,12},{5,1},{9,5},{13,9},{1,13},{6,2},{10,6},{... | collective-permute-start | bytes 122888 | tf_op jit(solution)/shard_map/ppermute | solution.py:18
  118.6 12.1 %collective-permute-start.30 = (f32[2,1,20,256]{3,0,2,1:T(2,128)S(1)}, f32[2,1,20,256]{3,0,2,1:T(2,128)S(1)}, u32[]{:S(2)}, u32[]{:S(2)}) collective-permute-start(f32[2,1,20,256]{3,0,2,1:T(2,128)S(1)} %get-tuple-element.22), channel_id=1, source_target_pairs={{0,4},{4,8},{8,12},{12,0},{1,5},{5,9},{9,13},{13,1},{2,6},{6,10},{... | collective-permute-start | bytes 122888 | tf_op jit(solution)/shard_map/ppermute | solution.py:17
  118.6 12.0 %collective-permute-start.31 = (f32[2,1,20,256]{3,0,2,1:T(2,128)S(1)}, f32[2,1,20,256]{3,0,2,1:T(2,128)S(1)}, u32[]{:S(2)}, u32[]{:S(2)}) collective-permute-start(f32[2,1,20,256]{3,0,2,1:T(2,128)S(1)} %get-tuple-element.23), channel_id=1, source_target_pairs={{4,0},{8,4},{12,8},{0,12},{5,1},{9,5},{13,9},{1,13},{6,2},{10,6},{... | collective-permute-start | bytes 122888 | tf_op jit(solution)/shard_map/ppermute | solution.py:18
  125.9 8.5 %collective-permute-start.16 = (f32[2,10,1,256]{3,0,2,1:T(2,128)S(1)}, f32[2,10,1,256]{3,0,2,1:T(2,128)S(1)}, u32[]{:S(2)}, u32[]{:S(2)}) collective-permute-start(f32[2,10,1,256]{3,0,2,1:T(2,128)S(1)} %get-tuple-element.15), channel_id=1, source_target_pairs={{2,0},{0,2},{3,1},{1,3},{6,4},{4,6},{7,5},{5,7},{10,8},{8,10},{11,... | collective-permute-start | bytes 61448 | tf_op jit(solution)/shard_map/ppermute | solution.py:18
  133.0 8.6 %collective-permute-start.17 = (f32[2,10,1,256]{3,0,2,1:T(2,128)S(1)}, f32[2,10,1,256]{3,0,2,1:T(2,128)S(1)}, u32[]{:S(2)}, u32[]{:S(2)}) collective-permute-start(f32[2,10,1,256]{3,0,2,1:T(2,128)S(1)} %get-tuple-element.14), channel_id=1, source_target_pairs={{0,2},{2,0},{1,3},{3,1},{4,6},{6,4},{5,7},{7,5},{8,10},{10,8},{9,1... | collective-permute-start | bytes 61448 | tf_op jit(solution)/shard_map/ppermute | solution.py:17
  (40 other events, 306.0 us)
Sparse Core Ops, SparseCore 0:
  141.7 4.8 reduce-scatter.1
where the time goes:
time: 156 us
  starting transfers between devices  64.3 us (41%)
  other arithmetic  43 us (28%)
  matrix products  25.3 us (16%)
  between operations  15.2 us (10%)
  local copies, waits for them, and re-layouts  6.65 us (4%)
    ppermute x16, starting transfers between devices, with_halo(): after = lax.ppermute(first, axis, down)  41.5 us
    ppermute x15, starting transfers between devices, with_halo(): before = lax.ppermute(last, axis, up)  21.2 us
    sub x7, other arithmetic, combine(): -mu * center[0] + bh[2] * right[0] + bh[3] * right[1] + bv[2] * down[0]  15.4 us
    sub x7, other arithmetic, combine(): mu * center[1] + bh[0] * right[0] + bh[1] * right[1] + bv[0] * down[0]  15.3 us
    dot_general x4, matrix products, pair_grad(): jnp.einsum('aijk,bijk->abij', val, lam_r, precision=hp)  6.78 us
    dot_general x4, matrix products, pair_grad(): jnp.einsum('aijk,bijk->abij', val, lam_d, precision=hp)  6.32 us
    dot_general x4, matrix products, pair_grad(): jnp.einsum('aijk,bijk->abij', lam, val_d, precision=hp)  6.18 us
    dot_general x4, matrix products, pair_grad(): jnp.einsum('aijk,bijk->abij', lam, val_r, precision=hp)  5.82 us
  transfers between devices with their start and end apart: 34, of which 2 were waited for; matrix products, arithmetic and copies ran while one was open for 46% of the time, Pallas kernels for 0%

commit v1 on v0

v1 whole, which is shorter than its diff:
```python
import functools

import jax
import jax.numpy as jnp
from jax import lax
from jax.experimental import pallas as pl
from jax.experimental.pallas import tpu as pltpu
from jax.sharding import PartitionSpec as P

half_step = 0.05
DEPTH = 4
MESH = pl.DeviceIdType.MESH
ROW_SIDES = ((-1, 0), (1, 0))
COL_SIDES = ((0, -1), (0, 1))
CORNERS = ((-1, -1), (-1, 1), (1, -1), (1, 1))
SIDES = ROW_SIDES + COL_SIDES + CORNERS
X0, Y0, X1, Y1, L2, LY1, L1, LY0 = range(8)


def kernel(
    sizes, x_hbm, c_hbm, onsite_ref, class_ref, table_ref, occ_ref,
    out_ref, grad_ref,
    own, fields, cf, tab, acc, part, part_in,
    send_rows, recv_rows, send_cols, recv_cols, send_corn, recv_corn,
    meta, meta_in, meta_pad,
    copy_sem, send_sem, recv_sem,
):
    gy_n, gx_n, orb_n, rows, cols, width = sizes
    halves = width // 128
    gy, gx, orb = lax.axis_index("gy"), lax.axis_index("gx"), lax.axis_index("orb")
    d = DEPTH
    left0 = 8 - d
    tail = cols - 16

    def at(si, sj):
        return {
            "gy": lax.rem(gy + si + gy_n, gy_n),
            "gx": lax.rem(gx + sj + gx_n, gx_n),
        }

    other = {"orb": lax.rem(orb + 1, orb_n)}

    loads = [
        pltpu.make_async_copy(src, own.at[f], copy_sem.at[f])
        for f, src in enumerate((x_hbm, c_hbm))
    ]
    for load in loads:
        load.start()

    barrier = pltpu.get_barrier_semaphore()
    for si, sj in SIDES:
        pl.semaphore_signal(barrier, inc=1, device_id=at(si, sj), device_id_type=MESH)
    pl.semaphore_signal(barrier, inc=1, device_id=other, device_id_type=MESH)

    meta[0:rows, 0:cols] = class_ref[0].astype(jnp.float32)
    meta[rows : 2 * rows, 0:cols] = class_ref[1].astype(jnp.float32)
    meta[2 * rows : 3 * rows, 0:cols] = half_step * onsite_ref[...]
    sign = (2 * occ_ref[...] - 1).astype(jnp.float32)

    zero = jnp.zeros((16, 128), jnp.float32)
    for e in range(4):
        t = jnp.broadcast_to(half_step * table_ref[:, e : e + 1], (16, 128))
        high = t.astype(jnp.bfloat16)
        rest = t - high.astype(jnp.float32)
        mid = rest.astype(jnp.bfloat16)
        low = (rest - mid.astype(jnp.float32)).astype(jnp.bfloat16)
        lanes = slice(e * 128, e * 128 + 128)
        tab[0:16, lanes] = high
        tab[16:32, lanes] = mid
        tab[32:48, lanes] = low
        tab[48:64, lanes] = zero.astype(jnp.bfloat16)
    tab[0:48, 512:640] = jnp.zeros((48, 128), jnp.bfloat16)
    tab[48:64, 512:640] = jnp.ones((16, 128), jnp.bfloat16)

    def pack(f, scale):
        def rows_of(side, first):
            def body(q, carry):
                for c in range(2):
                    v = own[f, c, first + q] * scale
                    send_rows[f, side, q, 16 * c : 16 * c + 16, :] = v[0:16]
                    send_rows[f, side, q, 32 + d * c : 32 + d * c + d, :] = v[16:cols]
                return carry

            lax.fori_loop(0, d, body, 0)

        rows_of(0, rows - d)
        rows_of(1, 0)

        def cols_of(i, carry):
            for c in range(2):
                v = own[f, c, i] * scale
                send_cols[f, 0, i, d * c : d * c + d, :] = v[cols - d : cols]
                send_cols[f, 1, i, d * c : d * c + d, :] = v[0:d]
            return carry

        lax.fori_loop(0, rows, cols_of, 0)

        def corners_of(q, carry):
            for k, (si, sj) in enumerate(CORNERS):
                i = q + (rows - 3 if si < 0 else 0)
                send_corn[f, k, q, :, :] = send_cols[f, 0 if sj < 0 else 1, i]
            return carry

        lax.fori_loop(0, 3, corners_of, 0)

    def remote(src, dst, n, to):
        return pltpu.make_async_remote_copy(
            src_ref=src, dst_ref=dst, send_sem=send_sem.at[n], recv_sem=recv_sem.at[n],
            device_id=to, device_id_type=MESH,
        )

    def field_copies(f):
        copies = []
        for k, (si, sj) in enumerate(ROW_SIDES):
            copies.append(remote(send_rows.at[f, k], recv_rows.at[f, k], 8 * f + k, at(-si, -sj)))
        for k, (si, sj) in enumerate(CORNERS):
            copies.append(remote(send_corn.at[f, k], recv_corn.at[f, k], 8 * f + 4 + k, at(-si, -sj)))
        for k, (si, sj) in enumerate(COL_SIDES):
            copies.append(remote(send_cols.at[f, k], recv_cols.at[f, k], 8 * f + 2 + k, at(-si, -sj)))
        return copies

    meta_copies = [
        remote(meta, meta_in.at[k], 16 + k, at(-si, -sj)) for k, (si, sj) in enumerate(SIDES)
    ]
    copies = [field_copies(0), field_copies(1)]

    loads[0].wait()
    pack(0, 1.0)
    pl.semaphore_wait(barrier, len(SIDES) + 1)
    for copy in meta_copies + copies[0]:
        copy.start()
    loads[1].wait()
    pack(1, sign)
    for copy in copies[1]:
        copy.start()

    def place_own(f, dst, scale):
        def body(i, carry):
            for c in range(2):
                fields[dst, c, d + i, 8 : 8 + cols, :] = own[f, c, i] * scale
            return carry

        lax.fori_loop(0, rows, body, 0)

    place_own(0, X0, 1.0)
    place_own(1, L2, sign)

    for copy in meta_copies:
        copy.wait()
    lane = lax.broadcasted_iota(jnp.int32, (3 * rows, 128), 1)

    def widened(west, middle, east):
        w = pltpu.roll(west, 128 - (cols - 8), 1)
        m = pltpu.roll(middle, 8, 1)
        e = pltpu.roll(east, 8 + cols, 1)
        return jnp.where(lane < 8, w, jnp.where(lane < 8 + cols, m, e))

    slot = {side: k for k, side in enumerate(SIDES)}
    for g, si in enumerate((-1, 0, 1)):
        middle = meta[...] if si == 0 else meta_in[slot[si, 0]]
        wide = widened(meta_in[slot[si, -1]], middle, meta_in[slot[si, 1]])
        for p in range(3):
            meta_pad[p, g * rows : (g + 1) * rows, :] = wide[p * rows : (p + 1) * rows]

    which = lax.broadcasted_iota(jnp.int32, (64, 128), 0)
    class_of = (which % 16).astype(jnp.float32)

    def coefficients(r, carry):
        line = pl.ds(rows - d + r, 1)
        mu = meta_pad[2, line, :]
        high = mu.astype(jnp.bfloat16).astype(jnp.float32)
        mid = (mu - high).astype(jnp.bfloat16).astype(jnp.float32)
        low = mu - high - mid
        hot = jnp.where(meta_pad[0, line, :] == class_of, 1.0, 0.0)
        parts = jnp.where(which == 48, high, jnp.where(which == 49, mid, jnp.where(which == 50, low, 0.0)))
        lhs = jnp.where(which < 48, hot, parts).astype(jnp.bfloat16)[:, 0:32]
        dims = (((0,), (0,)), ((), ()))
        got = lax.dot_general(lhs, tab[...], dims, preferred_element_type=jnp.float32)
        for e in range(4):
            cf[1 + e, r] = got[:, e * 128 : e * 128 + 128]
        cf[0, r] = got[:, 512:640]
        hot = jnp.where((meta_pad[1, line, :] == class_of) & (which < 48), 1.0, 0.0)
        lhs = hot.astype(jnp.bfloat16)[:, 0:32]
        got = lax.dot_general(lhs, tab[:, 0:512], dims, preferred_element_type=jnp.float32)
        for e in range(4):
            cf[5 + e, r] = got[:, e * 128 : e * 128 + 128]
        return carry

    lax.fori_loop(0, rows + 2 * d, coefficients, 0)

    def place_halo(f, dst):
        def cols_in(i, carry):
            for c in range(2):
                piece = slice(d * c, d * c + d)
                fields[dst, c, d + i, left0:8, :] = recv_cols[f, 0, i, piece, :]
                fields[dst, c, d + i, 8 + cols : 8 + cols + d, :] = recv_cols[f, 1, i, piece, :]
            return carry

        lax.fori_loop(0, rows, cols_in, 0)

        def rows_in(q, carry):
            for k, base in ((0, 0), (1, d + rows)):
                for c in range(2):
                    fields[dst, c, base + q, 8:24, :] = recv_rows[f, k, q, 16 * c : 16 * c + 16, :]
                    fields[dst, c, base + q, 24 : 8 + cols, :] = recv_rows[
                        f, k, q, 32 + d * c : 32 + d * c + d, :
                    ]
            return carry

        lax.fori_loop(0, d, rows_in, 0)

        def corners_in(q, carry):
            for k, (si, sj) in enumerate(CORNERS):
                r = q + (1 if si < 0 else d + rows)
                first = left0 if sj < 0 else 8 + cols
                for c in range(2):
                    fields[dst, c, r, first : first + d, :] = recv_corn[f, k, q, d * c : d * c + d, :]
            return carry

        lax.fori_loop(0, 3, corners_in, 0)

    def apply(src, first, last, emit):
        def body(r, carry):
            for h in range(halves):
                lanes = slice(h * 128, h * 128 + 128)
                c0, c1 = fields[src, 0, r, :, lanes], fields[src, 1, r, :, lanes]
                d0, d1 = fields[src, 0, r + 1, :, lanes], fields[src, 1, r + 1, :, lanes]
                u0, u1 = fields[src, 0, r - 1, :, lanes], fields[src, 1, r - 1, :, lanes]
                r0, r1 = pltpu.roll(c0, 31, 0), pltpu.roll(c1, 31, 0)
                mu = cf[0, r]
                b = [cf[1 + e, r] for e in range(4)]
                v = [cf[5 + e, r] for e in range(4)]
                p = [cf[5 + e, r - 1] for e in range(4)]
                w0 = mu * c1 + b[0] * r0 + b[1] * r1 + v[0] * d0 + v[1] * d1
                w0 = w0 - (p[0] * u0 + p[2] * u1) - pltpu.roll(b[0] * c0 + b[2] * c1, 1, 0)
                w1 = b[2] * r0 + b[3] * r1 + v[2] * d0 + v[3] * d1 - mu * c0
                w1 = w1 - (p[1] * u0 + p[3] * u1) - pltpu.roll(b[1] * c0 + b[3] * c1, 1, 0)
                emit(r, lanes, (w0, w1))
            return carry

        lax.fori_loop(first, last, body, 0)

    def plus(dst, base, factor):
        def emit(r, lanes, w):
            for c in range(2):
                moved = w[c] + w[c] if factor == 2 else w[c]
                fields[dst, c, r, :, lanes] = fields[base, c, r, :, lanes] + moved
        return emit

    def minus_twice(dst):
        def emit(r, lanes, w):
            for c in range(2):
                fields[dst, c, r, :, lanes] = -2.0 * w[c]
        return emit

    def closing(dst, base, mid):
        def emit(r, lanes, w):
            for c in range(2):
                fields[dst, c, r, :, lanes] = (
                    fields[base, c, r, :, lanes] + fields[mid, c, r, :, lanes] - w[c]
                )
        return emit

    def start_of(r, lanes, w):
        for c in range(2):
            whole = fields[L1, c, r, :, lanes] + fields[LY0, c, r, :, lanes] - w[c]
            out_ref[c, r - d, :, lanes] = whole[8 : 8 + cols]

    end = d + rows
    for copy in copies[0]:
        copy.wait()
    place_halo(0, X0)
    apply(X0, d - 2, end + 3, plus(Y0, X0, 1))
    apply(Y0, d - 1, end + 2, plus(X1, X0, 2))
    apply(X1, d, end + 1, plus(Y1, X1, 1))

    for copy in copies[1]:
        copy.wait()
    place_halo(1, L2)
    apply(L2, d - 3, end + 3, minus_twice(LY1))
    apply(LY1, d - 2, end + 2, closing(L1, L2, LY1))
    apply(L1, d - 1, end + 1, minus_twice(LY0))
    apply(LY0, d, end, start_of)

    own_lines = slice(8, 32)

    def gradient(i, carry):
        r = d + i
        sums = [jnp.zeros((24, 128), jnp.float32) for _ in range(8)]
        for h in range(halves):
            lanes = slice(h * 128, h * 128 + 128)
            for lam, val, twice in ((L2, Y1, True), (LY1, X1, False), (L1, Y0, True), (LY0, X0, False)):
                l = [fields[lam, c, r, own_lines, lanes] for c in range(2)]
                v = [fields[val, c, r, own_lines, lanes] for c in range(2)]
                ld = [fields[lam, c, r + 1, own_lines, lanes] for c in range(2)]
                vd = [fields[val, c, r + 1, own_lines, lanes] for c in range(2)]
                if twice:
                    l = [x + x for x in l]
                    ld = [x + x for x in ld]
                lr = [pltpu.roll(x, 23, 0) for x in l]
                vr = [pltpu.roll(x, 23, 0) for x in v]
                for a in range(2):
                    for b in range(2):
                        e = 2 * a + b
                        sums[e] = sums[e] + (l[a] * vr[b] - v[a] * lr[b])
                        sums[4 + e] = sums[4 + e] + (l[a] * vd[b] - v[a] * ld[b])
        for e in range(8):
            acc[e, i] = half_step * sums[e]
        return carry

    lax.fori_loop(0, rows, gradient, 0)

    total = jnp.zeros((8, 24 * rows), jnp.float32)
    entry = lax.broadcasted_iota(jnp.int32, (8, 128), 0)
    for e in range(8):
        chosen = jnp.where(entry == e, 1.0, 0.0)
        total = total + lax.dot_general(
            chosen, acc[e].reshape(24 * rows, 128), (((1,), (1,)), ((), ())),
            precision=lax.Precision.HIGHEST, preferred_element_type=jnp.float32,
        )
    part[...] = total
    swap = remote(part, part_in, 24, other)
    swap.start()
    swap.wait()
    total = part[...] + part_in[...]
    grad_ref[...] = jnp.where(orb == 0, total[0:4], total[4:8])


def on_device(sizes, checkpoint, cotangent, onsite, bond_class, bond_table, occupied):
    _, _, _, rows, cols, width = sizes
    d = DEPTH
    f32 = jnp.float32
    vmem = pl.BlockSpec(memory_space=pltpu.VMEM)
    hbm = pl.BlockSpec(memory_space=pl.ANY)
    start, grads = pl.pallas_call(
        functools.partial(kernel, sizes),
        out_shape=(
            jax.ShapeDtypeStruct(checkpoint.shape, f32),
            jax.ShapeDtypeStruct((4, 24 * rows), f32),
        ),
        in_specs=[hbm, hbm, vmem, vmem, vmem, vmem],
        out_specs=(vmem, vmem),
        scratch_shapes=[
            pltpu.VMEM((2, 2, rows, cols, width), f32),
            pltpu.VMEM((8, 2, rows + 2 * d, 32, width), f32),
            pltpu.VMEM((9, rows + 2 * d, 32, 128), f32),
            pltpu.VMEM((64, 640), jnp.bfloat16),
            pltpu.VMEM((8, rows, 24, 128), f32),
            pltpu.VMEM((8, 24 * rows), f32),
            pltpu.VMEM((8, 24 * rows), f32),
            pltpu.VMEM((2, 2, d, 2 * cols, width), f32),
            pltpu.VMEM((2, 2, d, 2 * cols, width), f32),
            pltpu.VMEM((2, 2, rows, 2 * d, width), f32),
            pltpu.VMEM((2, 2, rows, 2 * d, width), f32),
            pltpu.VMEM((2, 4, 3, 2 * d, width), f32),
            pltpu.VMEM((2, 4, 3, 2 * d, width), f32),
            pltpu.VMEM((3 * rows, 128), f32),
            pltpu.VMEM((8, 3 * rows, 128), f32),
            pltpu.VMEM((3, 3 * rows, 128), f32),
            pltpu.SemaphoreType.DMA((2,)),
            pltpu.SemaphoreType.DMA((25,)),
            pltpu.SemaphoreType.DMA((25,)),
        ],
        compiler_params=pltpu.CompilerParams(
            collective_id=0, has_side_effects=True, vmem_limit_bytes=40 * 1024 * 1024
        ),
        cost_estimate=pl.CostEstimate(flops=60_000_000, bytes_accessed=1_500_000, transcendentals=0),
    )(checkpoint, cotangent, onsite, bond_class, bond_table, occupied.reshape(1, width))
    return start, grads.reshape(4, rows, 24)[:, :, :cols]


def solution(mesh):
    shape = mesh.shape

    def body(checkpoint, cotangent, onsite, bond_class, bond_table, occupied):
        _, rows, cols, width = checkpoint.shape
        sizes = (shape["gy"], shape["gx"], shape["orb"], rows, cols, width)
        return on_device(sizes, checkpoint, cotangent, onsite, bond_class, bond_table, occupied)

    in_specs = (
        P("groups", "gy", "gx", "orb"),
        P("groups", "gy", "gx", "orb"),
        P(("groups", "gy"), "gx"),
        P("groups", "gy", "gx"),
        P(),
        P(("groups", "orb")),
    )
    out_specs = (P("groups", "gy", "gx", "orb"), P(("groups", "orb"), "gy", "gx"))
    return jax.shard_map(body, mesh=mesh, in_specs=in_specs, out_specs=out_specs, check_vma=False)
```

time: 156 us -> 38.7 us (0.25)
  starting transfers between devices: 64.3 us -> 0 us
  other arithmetic: 43 us -> 0 us
  Pallas kernels: 0 us -> 33.7 us
  matrix products: 25.3 us -> 0 us
  between operations: 15.2 us -> 0.68 us
  local copies, waits for them, and re-layouts: 6.65 us -> 4.08 us
    ppermute x33 -> x0, starting transfers between devices: 64.2 us -> none  [the longest x16 41.5 us: with_halo(): after = lax.ppermute(first, axis, down)]
    pallas_call x0 -> x1, Pallas kernels: none -> 33.7 us  [on_device(): pl.pallas_call(functools.partial(kernel, sizes), out_shape=(jax.ShapeDtyp...]
    sub x16 -> x0, other arithmetic: 33 us -> none  [the longest x7 15.4 us: combine(): -mu * center[0] + bh[2] * right[0] + bh[3] * right[1] + bv[2] * down[0]]
    dot_general x17 -> x0, matrix products: 25.3 us -> none  [the longest x4 6.78 us: pair_grad(): jnp.einsum('aijk,bijk->abij', val, lam_r, precision=hp)]
    dot_general x8 -> x0, other arithmetic: 4.06 us -> none  [the longest x4 3.29 us: pair_grad(): jnp.einsum('aijk,bijk->abij', lam, val_r, precision=hp)]
    sub x8 -> x0, local copies, waits for them, and re-layouts: 2.82 us -> none  [the longest x4 2.01 us: pair_grad(): jnp.einsum('aijk,bijk->abij', lam, val_d, precision=hp)]
    add x4 -> x0, other arithmetic: 2.14 us -> none  [the longest x2 1.11 us: two_sections(): middle = field + first * moved]
    mul x5 -> x0, other arithmetic: 2.12 us -> none  [the longest x1 1.26 us: on_device(): l2 = cotangent * signs[None, None, None, :]]
  transfers between devices with their start and end apart: 34 -> 0, of which waited for: 2 -> 0; matrix products, arithmetic and copies ran while one was open for 46% -> 0% of each run, Pallas kernels for 0% -> 0%
where the time goes in v1:
time: 38.7 us; the launch traced here: 38.5 us
  Pallas kernels  33.7 us (87%)
  local copies, waits for them, and re-layouts  4.08 us (11%)
  between operations  0.68 us (2%)
    pallas_call x1, Pallas kernels, on_device(): pl.pallas_call(functools.partial(kernel, sizes), out_shape=(jax.ShapeDtyp...  33.7 us
    unnamed x12, local copies, waits for them, and re-layouts  3.39 us

profile of v1, /device:TPU:0, one launch (start us, length us, event | category | flops | bytes accessed | tf_op | source)
XLA Modules:
  0.0 38.5 jit_solution(7229452073580068296)
XLA Ops:
  0.6 0.8 %copy.10.table_ref = f32[16,4]{1,0:T(8,128)S(1)} copy(f32[16,4]{0,1:T(4,128)} %param.10) | data formatting | bytes 512 | tf_op args[4]
  1.4 0.0 copy-start.3
  1.4 1.1 %copy.8.x_hbm = f32[2,8,20,256]{3,2,1,0:T(8,128)S(1)} copy(f32[2,8,20,256]{3,1,2,0:T(8,128)} %param.6) | data formatting | bytes 655360 | tf_op args[0]
  2.5 0.0 copy-done.3
  2.5 0.0 copy-start
  2.5 0.0 copy-start.1
  2.6 0.0 copy-start.2
  2.6 0.1 copy.9.c_hbm
  2.7 0.6 %copy-done = s32[2,8,20]{2,1,0:T(8,128)S(1)} copy-done((s32[2,8,20]{2,1,0:T(8,128)S(1)}, s32[2,8,20]{2,1,0:T(8,128)}, u32[]{:S(2)}) %copy-start) | copy-done | bytes 1304
  3.2 0.0 copy-done.1
  3.2 0.0 copy-done.2
  3.2 33.7 %shard_map.77 = (f32[2,8,20,256]{3,2,1,0:T(8,128)S(1)}, f32[4,192]{1,0:T(4,128)S(1)}) custom-call(f32[2,8,20,256]{3,2,1,0:T(8,128)S(1)} %copy.8.x_hbm, f32[2,8,20,256]{3,2,1,0:T(8,128)S(1)} %copy.9.c_hbm, f32[8,20]{1,0:T(8,128)S(1)} %copy-done.1, s32[2,8,20]{2,1,0:T(8,128)S(1)} %copy-done, f32[16,4]{1,0:T(8,128)S(1)} %copy.10.table_ref, s32[1,256]{1,0:T(1,128)S(1)} %bitcast.2), custom_call_target="tpu_custom_call" | custom-call | flops 60000000 | bytes 1500000 | tf_op jit(solution)/shard_map/pallas_call | solution.py:335
  36.9 0.8 %copy.11 = f32[2,8,20,256]{3,1,2,0:T(8,128)} copy(f32[2,8,20,256]{3,2,1,0:T(8,128)S(1)} %get-tuple-element.6) | data formatting | bytes 655360
  37.8 0.7 %reshape.11 = f32[4,8,24]{2,1,0:T(8,128)} reshape(f32[4,192]{1,0:T(4,128)S(1)} %get-tuple-element.5) | data formatting | bytes 6144 | tf_op jit(solution)/shard_map/reshape | solution.py:369
Async XLA Ops:
  1.4 1.1 %copy-start.3 = (f32[2,8,20,256]{3,1,2,0:T(8,128)S(1)}, f32[2,8,20,256]{3,1,2,0:T(8,128)}, u32[]{:S(2)}) copy-start(f32[2,8,20,256]{3,1,2,0:T(8,128)} %param.7) | copy-start | bytes 983044
  2.5 0.7 %copy-start = (s32[2,8,20]{2,1,0:T(8,128)S(1)}, s32[2,8,20]{2,1,0:T(8,128)}, u32[]{:S(2)}) copy-start(s32[2,8,20]{2,1,0:T(8,128)} %class_ref.1) | copy-start | bytes 3844
  2.5 0.7 %copy-start.1 = (f32[8,20]{1,0:T(8,128)S(1)}, f32[8,20]{1,0:T(8,128)}, u32[]{:S(2)}) copy-start(f32[8,20]{1,0:T(8,128)} %onsite_ref.1) | copy-start | bytes 1924
  2.6 0.7 %copy-start.2 = (s32[256]{0:T(256)S(1)}, s32[256]{0:T(256)}, u32[]{:S(2)}) copy-start(s32[256]{0:T(256)} %param.11) | copy-start | bytes 3076

commit v2 on v1

v2 whole, which is shorter than its diff:
```python
import functools

import jax
import jax.numpy as jnp
from jax import lax
from jax.experimental import pallas as pl
from jax.experimental.pallas import tpu as pltpu
from jax.sharding import PartitionSpec as P

half_step = 0.05
DEPTH = 4
MESH = pl.DeviceIdType.MESH
SIDES = ((-1, 0), (1, 0), (0, -1), (0, 1))
X0, Y0, X1, Y1, L2, LY1, L1, LY0 = range(8)


def kernel(
    sizes, x_hbm, c_hbm, onsite_ref, class_ref, table_ref, occ_ref,
    out_ref, grad_ref,
    own, fields, cf, tab, hot_ref, acc, part, part_in,
    send_rows, recv_rows, meta, meta_in, meta_mid, meta_side, meta_pad,
    copy_sem, send_sem, recv_sem,
):
    gy_n, gx_n, orb_n, rows, cols, width = sizes
    halves = width // 128
    gy, gx, orb = lax.axis_index("gy"), lax.axis_index("gx"), lax.axis_index("orb")
    d = DEPTH
    end = d + cols
    wide_cols = cols + 2 * d

    def at(si, sj):
        return {
            "gy": lax.rem(gy + si + gy_n, gy_n),
            "gx": lax.rem(gx + sj + gx_n, gx_n),
        }

    other_orb = lax.rem(orb + 1, orb_n)
    other = {"orb": other_orb}

    load_c = pltpu.make_async_copy(c_hbm, own, copy_sem.at[0])
    load_x = pltpu.make_async_copy(x_hbm, fields.at[X0, :, d:end, 0:8, :], copy_sem.at[1])
    load_c.start()
    load_x.start()

    barrier = pltpu.get_barrier_semaphore()
    for si, sj in SIDES:
        pl.semaphore_signal(barrier, inc=1, device_id=at(si, sj), device_id_type=MESH)
    pl.semaphore_signal(barrier, inc=1, device_id=other, device_id_type=MESH)

    meta[0:rows, 0:cols] = class_ref[0].astype(jnp.float32)
    meta[rows : 2 * rows, 0:cols] = class_ref[1].astype(jnp.float32)
    meta[2 * rows : 3 * rows, 0:cols] = half_step * onsite_ref[...]

    upper = lax.broadcasted_iota(jnp.int32, (8, width), 0) < 4

    def pack(f, j, c0, c1):
        turned = pltpu.roll(c1, 4, 0)
        send_rows[f, 0, j] = jnp.where(upper, c0, turned)
        send_rows[f, 1, j] = jnp.where(upper, turned, c0)

    def pack_c(j, carry):
        sign = (2 * occ_ref[...] - 1).astype(jnp.float32)
        c0, c1 = own[0, j] * sign, own[1, j] * sign
        fields[L2, 0, d + j, 0:8, :] = c0
        fields[L2, 1, d + j, 0:8, :] = c1
        pack(1, j, c0, c1)
        return carry

    def pack_x(j, carry):
        pack(0, j, fields[X0, 0, d + j, 0:8, :], fields[X0, 1, d + j, 0:8, :])
        return carry

    def remote(src, dst, n, to):
        return pltpu.make_async_remote_copy(
            src_ref=src, dst_ref=dst, send_sem=send_sem.at[n], recv_sem=recv_sem.at[n],
            device_id=to, device_id_type=MESH,
        )

    def field_copies(f, name):
        copies = []
        for k, si in ((0, 1), (1, -1)):
            copies.append(
                remote(send_rows.at[f, k], recv_rows.at[f, k, d:end], 8 * f + k, at(-si, 0))
            )
        mine = fields.at[name]
        copies.append(remote(
            mine.at[:, cols:end, 0:8, :], mine.at[:, 0:d, 0:8, :], 8 * f + 6, at(0, 1)
        ))
        copies.append(remote(
            mine.at[:, d : 2 * d, 0:8, :], mine.at[:, end : end + d, 0:8, :], 8 * f + 7, at(0, -1)
        ))
        return copies

    def corner_copies(f, k):
        got = recv_rows.at[f, k]
        return [
            remote(got.at[cols + 1 : end], got.at[1:d], 8 * f + 2 + k, at(0, 1)),
            remote(got.at[d : d + 3], got.at[end : end + 3], 8 * f + 4 + k, at(0, -1)),
        ]

    meta_copies = [
        remote(meta, meta_in.at[k], 16 + k, at(*to)) for k, to in enumerate(SIDES[:2])
    ]
    meta_wide = [
        remote(meta_mid, meta_side.at[k], 18 + k, at(*to)) for k, to in enumerate(SIDES[2:])
    ]
    copies_x, copies_c = field_copies(0, X0), field_copies(1, L2)

    load_c.wait()
    lax.fori_loop(0, cols, pack_c, 0)
    pl.semaphore_wait(barrier, len(SIDES) + 1)
    for copy in meta_copies + copies_c:
        copy.start()
    load_x.wait()
    lax.fori_loop(0, cols, pack_x, 0)
    for copy in copies_x:
        copy.start()

    diagonal = lax.broadcasted_iota(jnp.int32, (16, 16), 0) == lax.broadcasted_iota(
        jnp.int32, (16, 16), 1
    )
    blank = jnp.zeros((16, 128), jnp.bfloat16)
    for e in range(4):
        column = jnp.sum(jnp.where(diagonal, table_ref[e : e + 1, :], 0.0), axis=1, keepdims=True)
        t = jnp.broadcast_to(half_step * column, (16, 128))
        high = t.astype(jnp.bfloat16)
        rest = t - high.astype(jnp.float32)
        mid = rest.astype(jnp.bfloat16)
        lanes = slice(e * 128, e * 128 + 128)
        tab[0:16, lanes] = high
        tab[16:32, lanes] = mid
        tab[32:48, lanes] = (rest - mid.astype(jnp.float32)).astype(jnp.bfloat16)
        tab[48:64, lanes] = blank
    for n in range(3):
        tab[16 * n : 16 * n + 16, 512:640] = blank
    tab[48:64, 512:640] = jnp.ones((16, 128), jnp.bfloat16)

    for copy in meta_copies:
        copy.wait()
    upper_tile = lax.broadcasted_iota(jnp.int32, (8, 128), 0) < 4
    for p in range(3):
        of = slice(p * rows, (p + 1) * rows)
        meta_mid[p, 0:8, :] = meta[of]
        meta_mid[p, 8:16, :] = jnp.where(upper_tile, meta_in[0, of], meta_in[1, of])
    for copy in meta_wide:
        copy.start()
    for copy in meta_wide:
        copy.wait()
    lane = lax.broadcasted_iota(jnp.int32, (16, 128), 1)
    for p in range(3):
        west = pltpu.roll(meta_side[1, p], 128 - (cols - d), 1)
        east = pltpu.roll(meta_side[0, p], end, 1)
        middle = pltpu.roll(meta_mid[p], d, 1)
        meta_pad[p] = jnp.where(lane < d, west, jnp.where(lane < end, middle, east))

    which = lax.broadcasted_iota(jnp.int32, (16, 64), 1)
    class_of = (which % 16).astype(jnp.float32)
    for j in range(wide_cols):
        lines = slice(16 * j, 16 * j + 16)
        mu = meta_pad[2, :, j : j + 1]
        high = mu.astype(jnp.bfloat16).astype(jnp.float32)
        mid = (mu - high).astype(jnp.bfloat16).astype(jnp.float32)
        low = mu - high - mid
        hot = jnp.where(meta_pad[0, :, j : j + 1] == class_of, 1.0, 0.0)
        parts = jnp.where(
            which == 48, high, jnp.where(which == 49, mid, jnp.where(which == 50, low, 0.0))
        )
        hot_ref[0, lines, :] = jnp.where(which < 48, hot, parts).astype(jnp.bfloat16)
        hot = jnp.where((meta_pad[1, :, j : j + 1] == class_of) & (which < 48), 1.0, 0.0)
        hot_ref[1, lines, :] = hot.astype(jnp.bfloat16)

    def coefficients(q, carry):
        lines = pl.ds(pl.multiple_of(64 * q, 64), 64)
        got = jnp.dot(hot_ref[0, lines, :], tab[...], preferred_element_type=jnp.float32)
        for e in range(4):
            cf[1 + e, pl.ds(4 * q, 4)] = got[:, e * 128 : e * 128 + 128].reshape(4, 16, 128)
        cf[0, pl.ds(4 * q, 4)] = got[:, 512:640].reshape(4, 16, 128)
        got = jnp.dot(hot_ref[1, lines, :], tab[:, 0:512], preferred_element_type=jnp.float32)
        for e in range(4):
            cf[5 + e, pl.ds(4 * q, 4)] = got[:, e * 128 : e * 128 + 128].reshape(4, 16, 128)
        return carry

    lax.fori_loop(0, wide_cols // 4, coefficients, 0)

    def place_halo(f, name, first, last):
        def body(j, carry):
            below, above = recv_rows[f, 0, j], recv_rows[f, 1, j]
            fields[name, 0, j, 8:16, :] = jnp.where(upper, below, above)
            fields[name, 1, j, 8:16, :] = pltpu.roll(jnp.where(upper, above, below), 4, 0)
            return carry

        lax.fori_loop(first, last, body, 0)

    def apply(src, first, last, emit):
        def body(j, carry):
            for h in range(halves):
                lanes = slice(h * 128, h * 128 + 128)
                c0, c1 = fields[src, 0, j, :, lanes], fields[src, 1, j, :, lanes]
                r0, r1 = fields[src, 0, j + 1, :, lanes], fields[src, 1, j + 1, :, lanes]
                l0, l1 = fields[src, 0, j - 1, :, lanes], fields[src, 1, j - 1, :, lanes]
                d0, d1 = pltpu.roll(c0, 15, 0), pltpu.roll(c1, 15, 0)
                mu = cf[0, j]
                b = [cf[1 + e, j] for e in range(4)]
                p = [cf[1 + e, j - 1] for e in range(4)]
                v = [cf[5 + e, j] for e in range(4)]
                w0 = mu * c1 + b[0] * r0 + b[1] * r1 + v[0] * d0 + v[1] * d1
                w0 = w0 - (p[0] * l0 + p[2] * l1) - pltpu.roll(v[0] * c0 + v[2] * c1, 1, 0)
                w1 = b[2] * r0 + b[3] * r1 + v[2] * d0 + v[3] * d1 - mu * c0
                w1 = w1 - (p[1] * l0 + p[3] * l1) - pltpu.roll(v[1] * c0 + v[3] * c1, 1, 0)
                emit(j, lanes, (w0, w1))
            return carry

        lax.fori_loop(first, last, body, 0)

    def plus(dst, base, factor):
        def emit(j, lanes, w):
            for c in range(2):
                moved = w[c] + w[c] if factor == 2 else w[c]
                fields[dst, c, j, :, lanes] = fields[base, c, j, :, lanes] + moved
        return emit

    def minus_twice(dst):
        def emit(j, lanes, w):
            for c in range(2):
                fields[dst, c, j, :, lanes] = -2.0 * w[c]
        return emit

    def closing(dst, base, mid):
        def emit(j, lanes, w):
            for c in range(2):
                fields[dst, c, j, :, lanes] = (
                    fields[base, c, j, :, lanes] + fields[mid, c, j, :, lanes] - w[c]
                )
        return emit

    def start_of(j, lanes, w):
        for c in range(2):
            out_ref[c, j - d, :, lanes] = (
                fields[L1, c, j, 0:8, lanes] + fields[LY0, c, j, 0:8, lanes] - w[c][0:8]
            )

    def arrive(f, name, copies, step):
        corners = []
        for k in range(2):
            copies[k].wait_recv()
            sent = corner_copies(f, k)
            for copy in sent:
                copy.start()
            corners += sent
        place_halo(f, name, d, end)
        apply(name, d + 1, end - 1, step)
        for copy in copies[2:] + corners:
            copy.wait_recv()
        place_halo(f, name, 1, d)
        place_halo(f, name, end, end + 3)
        return corners

    step = minus_twice(LY1)
    corners_c = arrive(1, L2, copies_c, step)
    apply(L2, d - 3, d + 1, step)
    apply(L2, end - 1, end + 3, step)
    apply(LY1, d - 2, end + 2, closing(L1, L2, LY1))
    apply(L1, d - 1, end + 1, minus_twice(LY0))
    apply(LY0, d, end, start_of)

    step = plus(Y0, X0, 1)
    corners_x = arrive(0, X0, copies_x, step)
    apply(X0, d - 2, d + 1, step)
    apply(X0, end - 1, end + 3, step)
    apply(Y0, d - 1, end + 2, plus(X1, X0, 2))
    apply(X1, d, end + 1, plus(Y1, X1, 1))
    for copy in copies_c + corners_c + copies_x + corners_x:
        copy.wait_send()

    def gradient(i, carry):
        j = d + i
        sums = [jnp.zeros((8, 128), jnp.float32) for _ in range(8)]
        for h in range(halves):
            lanes = slice(h * 128, h * 128 + 128)
            for lam, val, twice in (
                (L2, Y1, True), (LY1, X1, False), (L1, Y0, True), (LY0, X0, False)
            ):
                l = [fields[lam, c, j, 0:8, lanes] for c in range(2)]
                v = [fields[val, c, j, 0:8, lanes] for c in range(2)]
                ld = [fields[lam, c, j, 1:9, lanes] for c in range(2)]
                vd = [fields[val, c, j, 1:9, lanes] for c in range(2)]
                lr = [fields[lam, c, j + 1, 0:8, lanes] for c in range(2)]
                vr = [fields[val, c, j + 1, 0:8, lanes] for c in range(2)]
                if twice:
                    v, vd, vr = ([x + x for x in group] for group in (v, vd, vr))
                for a in range(2):
                    for b in range(2):
                        e = 2 * a + b
                        sums[e] = sums[e] + (l[a] * vr[b] - v[a] * lr[b])
                        sums[4 + e] = sums[4 + e] + (l[a] * vd[b] - v[a] * ld[b])
        for e in range(8):
            acc[e, i] = sums[e]
        return carry

    lax.fori_loop(0, cols, gradient, 0)

    place = lax.broadcasted_iota(jnp.int32, (8, 128), 1)
    for e in range(8):
        total = jnp.zeros((8, 128), jnp.float32)
        for j in range(cols):
            total = jnp.where(place == j, jnp.sum(acc[e, j], axis=1, keepdims=True), total)
        part[e] = half_step * total
    swap = remote(part.at[pl.ds(4 * other_orb, 4)], part_in, 24, other)
    swap.start()
    swap.wait()
    total = part[pl.ds(4 * orb, 4)] + part_in[...]
    grad_ref[...] = total[:, :, 0:cols]


def on_device(sizes, checkpoint, cotangent, onsite, bond_class, bond_table, occupied):
    _, _, _, rows, cols, width = sizes
    d = DEPTH
    f32 = jnp.float32
    vmem = pl.BlockSpec(memory_space=pltpu.VMEM)
    hbm = pl.BlockSpec(memory_space=pl.ANY)
    start, grads = pl.pallas_call(
        functools.partial(kernel, sizes),
        out_shape=(
            jax.ShapeDtypeStruct((2, cols, rows, width), f32),
            jax.ShapeDtypeStruct((4, rows, cols), f32),
        ),
        in_specs=[hbm, hbm, vmem, vmem, vmem, vmem],
        out_specs=(vmem, vmem),
        scratch_shapes=[
            pltpu.VMEM((2, cols, rows, width), f32),
            pltpu.VMEM((8, 2, cols + 2 * d, 16, width), f32),
            pltpu.VMEM((9, cols + 2 * d, 16, 128), f32),
            pltpu.VMEM((64, 640), jnp.bfloat16),
            pltpu.VMEM((2, 16 * (cols + 2 * d), 64), jnp.bfloat16),
            pltpu.VMEM((8, cols, 8, 128), f32),
            pltpu.VMEM((8, 8, 128), f32),
            pltpu.VMEM((4, 8, 128), f32),
            pltpu.VMEM((2, 2, cols, 8, width), f32),
            pltpu.VMEM((2, 2, cols + 2 * d, 8, width), f32),
            pltpu.VMEM((3 * rows, 128), f32),
            pltpu.VMEM((2, 3 * rows, 128), f32),
            pltpu.VMEM((3, 16, 128), f32),
            pltpu.VMEM((2, 3, 16, 128), f32),
            pltpu.VMEM((3, 16, 128), f32),
            pltpu.SemaphoreType.DMA((2,)),
            pltpu.SemaphoreType.DMA((25,)),
            pltpu.SemaphoreType.DMA((25,)),
        ],
        compiler_params=pltpu.CompilerParams(
            collective_id=0, has_side_effects=True, vmem_limit_bytes=40 * 1024 * 1024
        ),
        cost_estimate=pl.CostEstimate(flops=60_000_000, bytes_accessed=1_500_000, transcendentals=0),
    )(
        checkpoint.transpose(0, 2, 1, 3), cotangent.transpose(0, 2, 1, 3), onsite, bond_class,
        bond_table.T, occupied.reshape(1, width),
    )
    return start.transpose(0, 2, 1, 3), grads


def solution(mesh):
    shape = mesh.shape

    def body(checkpoint, cotangent, onsite, bond_class, bond_table, occupied):
        _, rows, cols, width = checkpoint.shape
        sizes = (shape["gy"], shape["gx"], shape["orb"], rows, cols, width)
        return on_device(sizes, checkpoint, cotangent, onsite, bond_class, bond_table, occupied)

    in_specs = (
        P("groups", "gy", "gx", "orb"),
        P("groups", "gy", "gx", "orb"),
        P(("groups", "gy"), "gx"),
        P("groups", "gy", "gx"),
        P(),
        P(("groups", "orb")),
    )
    out_specs = (P("groups", "gy", "gx", "orb"), P(("groups", "orb"), "gy", "gx"))
    return jax.shard_map(body, mesh=mesh, in_specs=in_specs, out_specs=out_specs, check_vma=False)
```

time: 38.7 us -> 34.9 us (0.902)
  Pallas kernels: 33.7 us -> 29.3 us
  local copies, waits for them, and re-layouts: 4.08 us -> 4.66 us
    pallas_call x1, Pallas kernels: 33.7 us -> 29.3 us  [on_device(): pl.pallas_call(functools.partial(kernel, sizes), out_shape=(jax.ShapeDtyp...]
    unnamed x12 -> x14, local copies, waits for them, and re-layouts: 3.39 us -> 4.66 us
    reshape x1 -> x0, local copies, waits for them, and re-layouts: 0.68 us -> none  [on_device(): return (start, grads.reshape(4, rows, 24)[:, :, :cols])]
where the time goes in v2:
time: 34.9 us; the launch traced here: 34.6 us
  Pallas kernels  29.3 us (84%)
  local copies, waits for them, and re-layouts  4.66 us (13%)
  between operations  0.67 us (2%)
    pallas_call x1, Pallas kernels, on_device(): pl.pallas_call(functools.partial(kernel, sizes), out_shape=(jax.ShapeDtyp...  29.3 us
    unnamed x14, local copies, waits for them, and re-layouts  4.66 us

profile of v2, /device:TPU:0, one launch (start us, length us, event | category | flops | bytes accessed | tf_op | source)
XLA Modules:
  0.0 34.6 jit_solution(5727439385386676763)
XLA Ops:
  0.6 0.0 copy-start.3
  0.6 0.0 copy-start.4
  0.7 0.0 copy-start.5
  0.7 0.7 %copy-done.3 = f32[8,20]{1,0:T(8,128)S(1)} copy-done((f32[8,20]{1,0:T(8,128)S(1)}, f32[8,20]{1,0:T(8,128)}, u32[]{:S(2)}) %copy-start.3) | copy-done | bytes 664
  1.3 0.0 copy-done.4
  1.3 0.0 copy-done.5
  1.3 0.0 copy-start
  1.3 1.0 %copy-done = f32[2,8,20,256]{3,1,2,0:T(8,128)S(1)} copy-done((f32[2,8,20,256]{3,1,2,0:T(8,128)S(1)}, f32[2,8,20,256]{3,1,2,0:T(8,128)}, u32[]{:S(2)}) %copy-start) | copy-done | bytes 327704
  2.3 0.0 copy-start.1
  2.3 1.0 %copy-done.1 = f32[2,8,20,256]{3,1,2,0:T(8,128)S(1)} copy-done((f32[2,8,20,256]{3,1,2,0:T(8,128)S(1)}, f32[2,8,20,256]{3,1,2,0:T(8,128)}, u32[]{:S(2)}) %copy-start.1) | copy-done | bytes 327704
  3.3 0.0 copy-start.2
  3.3 0.7 %copy-done.2 = s32[2,8,20]{2,1,0:T(8,128)S(1)} copy-done((s32[2,8,20]{2,1,0:T(8,128)S(1)}, s32[2,8,20]{2,1,0:T(8,128)}, u32[]{:S(2)}) %copy-start.2) | copy-done | bytes 1304
  4.0 29.3 %shard_map.77 = (f32[2,20,8,256]{3,2,1,0:T(8,128)S(1)}, f32[4,8,20]{2,1,0:T(8,128)S(1)}) custom-call(f32[2,20,8,256]{3,2,1,0:T(8,128)S(1)} %bitcast.5, f32[2,20,8,256]{3,2,1,0:T(8,128)S(1)} %bitcast.6, f32[8,20]{1,0:T(8,128)S(1)} %copy-done.3, s32[2,8,20]{2,1,0:T(8,128)S(1)} %copy-done.2, f32[4,16]{1,0:T(4,128)S(1)} %bitcast.8, s32[1,256]{1,0:T(1,128)S(1)} %bitcast.9), custom_call_target="tpu_custom_call" | custom-call | flops 60000000 | bytes 1500000 | tf_op jit(solution)/shard_map/pallas_call | solution.py:321
  33.3 0.7 %copy.10 = f32[2,8,20,256]{3,1,2,0:T(8,128)} copy(f32[2,8,20,256]{3,1,2,0:T(8,128)S(1)} %bitcast.7) | data formatting | bytes 655360
  34.0 0.6 %copy.11 = f32[4,8,20]{2,1,0:T(8,128)} copy(f32[4,8,20]{2,1,0:T(8,128)S(1)} %get-tuple-element.9) | data formatting | bytes 5120
Async XLA Ops:
  0.6 0.7 %copy-start.3 = (f32[8,20]{1,0:T(8,128)S(1)}, f32[8,20]{1,0:T(8,128)}, u32[]{:S(2)}) copy-start(f32[8,20]{1,0:T(8,128)} %onsite_ref.1) | copy-start | bytes 1924
  0.6 0.7 %copy-start.4 = (f32[16,4]{0,1:T(4,128)S(1)}, f32[16,4]{0,1:T(4,128)}, u32[]{:S(2)}) copy-start(f32[16,4]{0,1:T(4,128)} %param.10) | copy-start | bytes 772
  0.7 0.7 %copy-start.5 = (s32[256]{0:T(256)S(1)}, s32[256]{0:T(256)}, u32[]{:S(2)}) copy-start(s32[256]{0:T(256)} %param.11) | copy-start | bytes 3076
  1.3 1.0 %copy-start = (f32[2,8,20,256]{3,1,2,0:T(8,128)S(1)}, f32[2,8,20,256]{3,1,2,0:T(8,128)}, u32[]{:S(2)}) copy-start(f32[2,8,20,256]{3,1,2,0:T(8,128)} %param.6) | copy-start | bytes 983044
  2.3 1.0 %copy-start.1 = (f32[2,8,20,256]{3,1,2,0:T(8,128)S(1)}, f32[2,8,20,256]{3,1,2,0:T(8,128)}, u32[]{:S(2)}) copy-start(f32[2,8,20,256]{3,1,2,0:T(8,128)} %param.7) | copy-start | bytes 983044
  3.3 0.7 %copy-start.2 = (s32[2,8,20]{2,1,0:T(8,128)S(1)}, s32[2,8,20]{2,1,0:T(8,128)}, u32[]{:S(2)}) copy-start(s32[2,8,20]{2,1,0:T(8,128)} %class_ref.1) | copy-start | bytes 3844

commit v3 on v2

--- a/solution.py
+++ b/solution.py
@@ -9,6 +9,7 @@
 
 half_step = 0.05
 DEPTH = 4
+ROW_SEM = 25
 MESH = pl.DeviceIdType.MESH
 SIDES = ((-1, 0), (1, 0), (0, -1), (0, 1))
 X0, Y0, X1, Y1, L2, LY1, L1, LY0 = range(8)
@@ -77,11 +78,14 @@
         )
 
     def field_copies(f, name):
-        copies = []
+        edges, copies = [], []
         for k, si in ((0, 1), (1, -1)):
-            copies.append(
-                remote(send_rows.at[f, k], recv_rows.at[f, k, d:end], 8 * f + k, at(-si, 0))
-            )
+            for n, (first, last) in enumerate(((0, 3), (cols - 3, cols), (3, cols - 3))):
+                copy = remote(
+                    send_rows.at[f, k, first:last], recv_rows.at[f, k, d + first : d + last],
+                    ROW_SEM + 6 * f + 3 * k + n, at(-si, 0),
+                )
+                (edges if n < 2 else copies).append(copy)
         mine = fields.at[name]
         copies.append(remote(
             mine.at[:, cols:end, 0:8, :], mine.at[:, 0:d, 0:8, :], 8 * f + 6, at(0, 1)
@@ -89,7 +93,7 @@
         copies.append(remote(
             mine.at[:, d : 2 * d, 0:8, :], mine.at[:, end : end + d, 0:8, :], 8 * f + 7, at(0, -1)
         ))
-        return copies
+        return edges, copies
 
     def corner_copies(f, k):
         got = recv_rows.at[f, k]
@@ -104,16 +108,16 @@
     meta_wide = [
         remote(meta_mid, meta_side.at[k], 18 + k, at(*to)) for k, to in enumerate(SIDES[2:])
     ]
-    copies_x, copies_c = field_copies(0, X0), field_copies(1, L2)
+    (edges_x, copies_x), (edges_c, copies_c) = field_copies(0, X0), field_copies(1, L2)
 
     load_c.wait()
     lax.fori_loop(0, cols, pack_c, 0)
     pl.semaphore_wait(barrier, len(SIDES) + 1)
-    for copy in meta_copies + copies_c:
+    for copy in meta_copies + edges_c:
         copy.start()
     load_x.wait()
     lax.fori_loop(0, cols, pack_x, 0)
-    for copy in copies_x:
+    for copy in edges_x + copies_c + copies_x:
         copy.start()
 
     diagonal = lax.broadcasted_iota(jnp.int32, (16, 16), 0) == lax.broadcasted_iota(
@@ -239,37 +243,36 @@
                 fields[L1, c, j, 0:8, lanes] + fields[LY0, c, j, 0:8, lanes] - w[c][0:8]
             )
 
-    def arrive(f, name, copies, step):
+    def forward(f, edges):
         corners = []
         for k in range(2):
-            copies[k].wait_recv()
+            for copy in edges[2 * k : 2 * k + 2]:
+                copy.wait_recv()
             sent = corner_copies(f, k)
             for copy in sent:
                 copy.start()
             corners += sent
-        place_halo(f, name, d, end)
-        apply(name, d + 1, end - 1, step)
-        for copy in copies[2:] + corners:
+        return corners
+
+    corners_c = forward(1, edges_c)
+    corners_x = forward(0, edges_x)
+
+    def arrive(f, name, copies, corners):
+        for copy in corners + copies:
             copy.wait_recv()
-        place_halo(f, name, 1, d)
-        place_halo(f, name, end, end + 3)
-        return corners
-
-    step = minus_twice(LY1)
-    corners_c = arrive(1, L2, copies_c, step)
-    apply(L2, d - 3, d + 1, step)
-    apply(L2, end - 1, end + 3, step)
+        place_halo(f, name, 1, wide_cols - 1)
+
+    arrive(1, L2, copies_c, corners_c)
+    apply(L2, d - 3, end + 3, minus_twice(LY1))
     apply(LY1, d - 2, end + 2, closing(L1, L2, LY1))
     apply(L1, d - 1, end + 1, minus_twice(LY0))
     apply(LY0, d, end, start_of)
 
-    step = plus(Y0, X0, 1)
-    corners_x = arrive(0, X0, copies_x, step)
-    apply(X0, d - 2, d + 1, step)
-    apply(X0, end - 1, end + 3, step)
+    arrive(0, X0, copies_x, corners_x)
+    apply(X0, d - 2, end + 3, plus(Y0, X0, 1))
     apply(Y0, d - 1, end + 2, plus(X1, X0, 2))
     apply(X1, d, end + 1, plus(Y1, X1, 1))
-    for copy in copies_c + corners_c + copies_x + corners_x:
+    for copy in edges_c + copies_c + corners_c + edges_x + copies_x + corners_x:
         copy.wait_send()
 
     def gradient(i, carry):
@@ -317,7 +320,7 @@
     d = DEPTH
     f32 = jnp.float32
     vmem = pl.BlockSpec(memory_space=pltpu.VMEM)
-    hbm = pl.BlockSpec(memory_space=pl.ANY)
+    hbm = pl.BlockSpec(memory_space=pltpu.HBM)
     start, grads = pl.pallas_call(
         functools.partial(kernel, sizes),
         out_shape=(
@@ -343,8 +346,8 @@
             pltpu.VMEM((2, 3, 16, 128), f32),
             pltpu.VMEM((3, 16, 128), f32),
             pltpu.SemaphoreType.DMA((2,)),
-            pltpu.SemaphoreType.DMA((25,)),
-            pltpu.SemaphoreType.DMA((25,)),
+            pltpu.SemaphoreType.DMA((ROW_SEM + 12,)),
+            pltpu.SemaphoreType.DMA((ROW_SEM + 12,)),
         ],
         compiler_params=pltpu.CompilerParams(
             collective_id=0, has_side_effects=True, vmem_limit_bytes=40 * 1024 * 1024

time: 34.9 us -> 33 us (0.946)
  Pallas kernels: 29.3 us -> 27.4 us
    pallas_call x1, Pallas kernels: 29.3 us -> 27.4 us  [on_device(): pl.pallas_call(functools.partial(kernel, sizes), out_shape=(jax.ShapeDtyp...]
where the time goes in v3:
time: 33 us; the launch traced here: 32.7 us
  Pallas kernels  27.4 us (83%)
  local copies, waits for them, and re-layouts  4.66 us (14%)
  between operations  0.67 us (2%)
    pallas_call x1, Pallas kernels, on_device(): pl.pallas_call(functools.partial(kernel, sizes), out_shape=(jax.ShapeDtyp...  27.4 us
    unnamed x14, local copies, waits for them, and re-layouts  4.66 us

profile of v3, /device:TPU:0, one launch (start us, length us, event | category | flops | bytes accessed | tf_op | source)
XLA Modules:
  0.0 32.7 jit_solution(3139130993949733665)
XLA Ops:
  0.6 0.0 copy-start.3
  0.6 0.0 copy-start.4
  0.7 0.0 copy-start.5
  0.7 0.7 %copy-done.3 = f32[8,20]{1,0:T(8,128)S(1)} copy-done((f32[8,20]{1,0:T(8,128)S(1)}, f32[8,20]{1,0:T(8,128)}, u32[]{:S(2)}) %copy-start.3) | copy-done | bytes 664
  1.3 0.0 copy-done.4
  1.3 0.0 copy-done.5
  1.3 0.0 copy-start
  1.3 1.0 %copy-done = f32[2,8,20,256]{3,1,2,0:T(8,128)S(1)} copy-done((f32[2,8,20,256]{3,1,2,0:T(8,128)S(1)}, f32[2,8,20,256]{3,1,2,0:T(8,128)}, u32[]{:S(2)}) %copy-start) | copy-done | bytes 327704
  2.3 0.0 copy-start.1
  2.3 1.0 %copy-done.1 = f32[2,8,20,256]{3,1,2,0:T(8,128)S(1)} copy-done((f32[2,8,20,256]{3,1,2,0:T(8,128)S(1)}, f32[2,8,20,256]{3,1,2,0:T(8,128)}, u32[]{:S(2)}) %copy-start.1) | copy-done | bytes 327704
  3.3 0.0 copy-start.2
  3.3 0.7 %copy-done.2 = s32[2,8,20]{2,1,0:T(8,128)S(1)} copy-done((s32[2,8,20]{2,1,0:T(8,128)S(1)}, s32[2,8,20]{2,1,0:T(8,128)}, u32[]{:S(2)}) %copy-start.2) | copy-done | bytes 1304
  4.0 27.4 %shard_map.77 = (f32[2,20,8,256]{3,2,1,0:T(8,128)S(1)}, f32[4,8,20]{2,1,0:T(8,128)S(1)}) custom-call(f32[2,20,8,256]{3,2,1,0:T(8,128)S(1)} %bitcast.5, f32[2,20,8,256]{3,2,1,0:T(8,128)S(1)} %bitcast.6, f32[8,20]{1,0:T(8,128)S(1)} %copy-done.3, s32[2,8,20]{2,1,0:T(8,128)S(1)} %copy-done.2, f32[4,16]{1,0:T(4,128)S(1)} %bitcast.8, s32[1,256]{1,0:T(1,128)S(1)} %bitcast.9), custom_call_target="tpu_custom_call" | custom-call | flops 60000000 | bytes 1500000 | tf_op jit(solution)/shard_map/pallas_call | solution.py:324
  31.4 0.7 %copy.10 = f32[2,8,20,256]{3,1,2,0:T(8,128)} copy(f32[2,8,20,256]{3,1,2,0:T(8,128)S(1)} %bitcast.7) | data formatting | bytes 655360
  32.1 0.6 %copy.11 = f32[4,8,20]{2,1,0:T(8,128)} copy(f32[4,8,20]{2,1,0:T(8,128)S(1)} %get-tuple-element.9) | data formatting | bytes 5120
Async XLA Ops:
  0.6 0.7 %copy-start.3 = (f32[8,20]{1,0:T(8,128)S(1)}, f32[8,20]{1,0:T(8,128)}, u32[]{:S(2)}) copy-start(f32[8,20]{1,0:T(8,128)} %onsite_ref.1) | copy-start | bytes 1924
  0.6 0.7 %copy-start.4 = (f32[16,4]{0,1:T(4,128)S(1)}, f32[16,4]{0,1:T(4,128)}, u32[]{:S(2)}) copy-start(f32[16,4]{0,1:T(4,128)} %param.10) | copy-start | bytes 772
  0.7 0.7 %copy-start.5 = (s32[256]{0:T(256)S(1)}, s32[256]{0:T(256)}, u32[]{:S(2)}) copy-start(s32[256]{0:T(256)} %param.11) | copy-start | bytes 3076
  1.3 1.0 %copy-start = (f32[2,8,20,256]{3,1,2,0:T(8,128)S(1)}, f32[2,8,20,256]{3,1,2,0:T(8,128)}, u32[]{:S(2)}) copy-start(f32[2,8,20,256]{3,1,2,0:T(8,128)} %param.6) | copy-start | bytes 983044
  2.3 1.0 %copy-start.1 = (f32[2,8,20,256]{3,1,2,0:T(8,128)S(1)}, f32[2,8,20,256]{3,1,2,0:T(8,128)}, u32[]{:S(2)}) copy-start(f32[2,8,20,256]{3,1,2,0:T(8,128)} %param.7) | copy-start | bytes 983044
  3.3 0.7 %copy-start.2 = (s32[2,8,20]{2,1,0:T(8,128)S(1)}, s32[2,8,20]{2,1,0:T(8,128)}, u32[]{:S(2)}) copy-start(s32[2,8,20]{2,1,0:T(8,128)} %class_ref.1) | copy-start | bytes 3844

commit v4 on v3

--- a/solution.py
+++ b/solution.py
@@ -214,7 +214,7 @@
                 emit(j, lanes, (w0, w1))
             return carry
 
-        lax.fori_loop(first, last, body, 0)
+        lax.fori_loop(first, last, body, 0, unroll=2)
 
     def plus(dst, base, factor):
         def emit(j, lanes, w):
@@ -300,7 +300,7 @@
             acc[e, i] = sums[e]
         return carry
 
-    lax.fori_loop(0, cols, gradient, 0)
+    lax.fori_loop(0, cols, gradient, 0, unroll=2)
 
     place = lax.broadcasted_iota(jnp.int32, (8, 128), 1)
     for e in range(8):

time: 33 us -> 32.3 us (0.979)
  Pallas kernels: 27.4 us -> 26.7 us
    pallas_call x1, Pallas kernels: 27.4 us -> 26.7 us  [on_device(): pl.pallas_call(functools.partial(kernel, sizes), out_shape=(jax.ShapeDtyp...]
where the time goes in v4:
time: 32.3 us; the launch traced here: 32.1 us
  Pallas kernels  26.7 us (83%)
  local copies, waits for them, and re-layouts  4.66 us (14%)
  between operations  0.67 us (2%)
    pallas_call x1, Pallas kernels, on_device(): pl.pallas_call(functools.partial(kernel, sizes), out_shape=(jax.ShapeDtyp...  26.7 us
    unnamed x14, local copies, waits for them, and re-layouts  4.66 us

profile of v4, /device:TPU:0, one launch (start us, length us, event | category | flops | bytes accessed | tf_op | source)
XLA Modules:
  0.0 32.1 jit_solution(11698147482717945968)
XLA Ops:
  0.6 0.0 copy-start.3
  0.6 0.0 copy-start.4
  0.7 0.0 copy-start.5
  0.7 0.7 %copy-done.3 = f32[8,20]{1,0:T(8,128)S(1)} copy-done((f32[8,20]{1,0:T(8,128)S(1)}, f32[8,20]{1,0:T(8,128)}, u32[]{:S(2)}) %copy-start.3) | copy-done | bytes 664
  1.3 0.0 copy-done.4
  1.3 0.0 copy-done.5
  1.3 0.0 copy-start
  1.3 1.0 %copy-done = f32[2,8,20,256]{3,1,2,0:T(8,128)S(1)} copy-done((f32[2,8,20,256]{3,1,2,0:T(8,128)S(1)}, f32[2,8,20,256]{3,1,2,0:T(8,128)}, u32[]{:S(2)}) %copy-start) | copy-done | bytes 327704
  2.3 0.0 copy-start.1
  2.3 1.0 %copy-done.1 = f32[2,8,20,256]{3,1,2,0:T(8,128)S(1)} copy-done((f32[2,8,20,256]{3,1,2,0:T(8,128)S(1)}, f32[2,8,20,256]{3,1,2,0:T(8,128)}, u32[]{:S(2)}) %copy-start.1) | copy-done | bytes 327704
  3.3 0.0 copy-start.2
  3.3 0.7 %copy-done.2 = s32[2,8,20]{2,1,0:T(8,128)S(1)} copy-done((s32[2,8,20]{2,1,0:T(8,128)S(1)}, s32[2,8,20]{2,1,0:T(8,128)}, u32[]{:S(2)}) %copy-start.2) | copy-done | bytes 1304
  4.0 26.7 %shard_map.77 = (f32[2,20,8,256]{3,2,1,0:T(8,128)S(1)}, f32[4,8,20]{2,1,0:T(8,128)S(1)}) custom-call(f32[2,20,8,256]{3,2,1,0:T(8,128)S(1)} %bitcast.5, f32[2,20,8,256]{3,2,1,0:T(8,128)S(1)} %bitcast.6, f32[8,20]{1,0:T(8,128)S(1)} %copy-done.3, s32[2,8,20]{2,1,0:T(8,128)S(1)} %copy-done.2, f32[4,16]{1,0:T(4,128)S(1)} %bitcast.8, s32[1,256]{1,0:T(1,128)S(1)} %bitcast.9), custom_call_target="tpu_custom_call" | custom-call | flops 60000000 | bytes 1500000 | tf_op jit(solution)/shard_map/pallas_call | solution.py:324
  30.7 0.7 %copy.10 = f32[2,8,20,256]{3,1,2,0:T(8,128)} copy(f32[2,8,20,256]{3,1,2,0:T(8,128)S(1)} %bitcast.7) | data formatting | bytes 655360
  31.5 0.6 %copy.11 = f32[4,8,20]{2,1,0:T(8,128)} copy(f32[4,8,20]{2,1,0:T(8,128)S(1)} %get-tuple-element.9) | data formatting | bytes 5120
Async XLA Ops:
  0.6 0.7 %copy-start.3 = (f32[8,20]{1,0:T(8,128)S(1)}, f32[8,20]{1,0:T(8,128)}, u32[]{:S(2)}) copy-start(f32[8,20]{1,0:T(8,128)} %onsite_ref.1) | copy-start | bytes 1924
  0.6 0.7 %copy-start.4 = (f32[16,4]{0,1:T(4,128)S(1)}, f32[16,4]{0,1:T(4,128)}, u32[]{:S(2)}) copy-start(f32[16,4]{0,1:T(4,128)} %param.10) | copy-start | bytes 772
  0.7 0.7 %copy-start.5 = (s32[256]{0:T(256)S(1)}, s32[256]{0:T(256)}, u32[]{:S(2)}) copy-start(s32[256]{0:T(256)} %param.11) | copy-start | bytes 3076
  1.3 1.0 %copy-start = (f32[2,8,20,256]{3,1,2,0:T(8,128)S(1)}, f32[2,8,20,256]{3,1,2,0:T(8,128)}, u32[]{:S(2)}) copy-start(f32[2,8,20,256]{3,1,2,0:T(8,128)} %param.6) | copy-start | bytes 983044
  2.3 1.0 %copy-start.1 = (f32[2,8,20,256]{3,1,2,0:T(8,128)S(1)}, f32[2,8,20,256]{3,1,2,0:T(8,128)}, u32[]{:S(2)}) copy-start(f32[2,8,20,256]{3,1,2,0:T(8,128)} %param.7) | copy-start | bytes 983044
  3.3 0.7 %copy-start.2 = (s32[2,8,20]{2,1,0:T(8,128)S(1)}, s32[2,8,20]{2,1,0:T(8,128)}, u32[]{:S(2)}) copy-start(s32[2,8,20]{2,1,0:T(8,128)} %class_ref.1) | copy-start | bytes 3844
